TPU v7x, 128 devices: a whole 4x4x4 slice. The times are simulated.
128 devices in a mesh: scene: 8 (over y, core), frame: 16 (over z, x).
Axes of the slice: x: 4, y: 4, z: 4, core: 2. Of those that a mesh axis runs over, the one named last changes fastest.
Arguments:
- occupancy: bfloat16 [8, 64, 64, 2048], P('scene', 'frame'), may hold values from -6 to 6
- scene_lengths: int32 [8], P('scene'), may hold values from 8 to 64, as said below
- conv1_weight: bfloat16 [128, 1728], replicated, may hold values from -0.15625 to 0.15625
- conv2_weight: bfloat16 [256, 3456], replicated, may hold values from -0.109375 to 0.109375
- temporal_weight: bfloat16 [3, 256, 256], replicated, may hold values from -0.21875 to 0.21875
- query_weight: bfloat16 [256, 256], replicated
- key_weight: bfloat16 [256, 256], replicated
- value_weight: bfloat16 [256, 256], replicated, may hold values from -0.375 to 0.375
- out_weight: bfloat16 [256, 256], replicated, may hold values from -0.375 to 0.375
Outputs:
- encoded: bfloat16 [8, 64, 256, 512], P('scene', 'frame')
- kl_loss: float32 [], replicated
Inputs may be any that keep to these rules, and one draw needn't show every extreme that they name: `scene_lengths`: non-decreasing along the scenes; the first scene has exactly 8 frames with data and the last exactly 64.
All inputs are finite; a program needn't handle non-finite values.
Results may differ from a plain program's by a relative error of at most 0.011.
Values may be sent and summed in bfloat16 or wider, within the bound.
A program may use at most 192 MiB of HBM per device.

v0:
```python
import jax
import jax.numpy as jnp
from jax import lax
from jax.sharding import PartitionSpec as P

CIN = 64
C1 = 128
C2 = 256
HEADS = 4
HD = 64
HI = 16
ZD = 8
CELLS = 512


NORM_EPS = 1e-06


def extended(cells, sides, width):
    for axis, dim in sides:
        count = lax.axis_size(axis)
        ends = count - 1
        head = lax.slice_in_dim(cells, 0, width, axis=dim)
        tail = lax.slice_in_dim(cells, cells.shape[dim] - width, cells.shape[dim], axis=dim)
        cells = jnp.concatenate(
            [
                lax.ppermute(tail, axis, [(i, (i + 1) % count) for i in range(ends)]),
                cells,
                lax.ppermute(head, axis, [((i + 1) % count, i) for i in range(ends)]),
            ],
            axis=dim,
        )
    return cells


def spatial_conv(voxels, weight, channels_in, stride):
    channels_out = weight.shape[0]
    kernel = weight.reshape(channels_out, channels_in, 3, 3, 3)
    return lax.conv_general_dilated(
        voxels,
        kernel,
        (stride, stride, 1),
        ((1, 1), (1, 1), (1, 1)),
        dimension_numbers=("NCDHW", "OIDHW", "NCDHW"),
        preferred_element_type=jnp.float32,
    )


def mix_channels(weight, maps):
    return jnp.einsum("oc,fcn->fon", weight, maps, preferred_element_type=jnp.float32)


def temporal_block(padded, second_maps, temporal_weight):
    count_frames = second_maps.shape[0]
    temporal_sum = mix_channels(temporal_weight[0], padded[0:count_frames])
    for tap in range(1, 3):
        temporal_sum = temporal_sum + mix_channels(
            temporal_weight[tap], padded[tap : tap + count_frames]
        )
    residual_maps = (second_maps.astype(jnp.float32) + jax.nn.silu(temporal_sum)).astype(
        jnp.bfloat16
    )
    return residual_maps.astype(jnp.float32)


def project_rows(residual_f, query_weight, key_weight, value_weight):
    count_frames = residual_f.shape[0]
    count_cells = residual_f.shape[2]
    normed = (
        residual_f * lax.rsqrt(jnp.mean(residual_f * residual_f, axis=1, keepdims=True) + NORM_EPS)
    ).astype(jnp.bfloat16)
    queries = (
        mix_channels(query_weight, normed)
        .astype(jnp.bfloat16)
        .reshape(count_frames, HEADS, HD, count_cells)
    )
    key_rows = (
        mix_channels(key_weight, normed)
        .astype(jnp.bfloat16)
        .reshape(count_frames, HEADS, HD, count_cells)
    )
    value_rows = (
        mix_channels(value_weight, normed)
        .astype(jnp.bfloat16)
        .reshape(count_frames, HEADS, HD, count_cells)
    )
    return (queries, key_rows, value_rows)


def finish_rows(residual_f, attended, out_weight, valid_rows):
    count_frames = residual_f.shape[0]
    count_cells = residual_f.shape[2]
    out_full = residual_f + mix_channels(
        out_weight, attended.reshape(count_frames, C2, count_cells)
    )
    return (out_full * valid_rows[:, None, None]).astype(jnp.bfloat16)


def shards(
    occupancy,
    scene_lengths,
    conv1_weight,
    conv2_weight,
    temporal_weight,
    query_weight,
    key_weight,
    value_weight,
    out_weight,
):
    f_dev = occupancy.shape[1]
    length = scene_lengths[0]
    first_frame = lax.axis_index("frame") * f_dev
    frame_ids = first_frame + jnp.arange(f_dev, dtype=jnp.int32)
    valid_rows = (frame_ids < length).astype(jnp.float32)
    voxels = occupancy[0].reshape(f_dev, CIN, HI, HI, ZD)
    first_maps = jax.nn.silu(spatial_conv(voxels, conv1_weight, CIN, 2)).astype(jnp.bfloat16)
    second_full = jax.nn.silu(spatial_conv(first_maps, conv2_weight, C1, 1))
    second_maps = (second_full.reshape(f_dev, C2, CELLS) * valid_rows[:, None, None]).astype(
        jnp.bfloat16
    )
    padded = extended(second_maps, (("frame", 0),), 1)
    residual_f = temporal_block(padded, second_maps, temporal_weight)
    queries, key_rows, value_rows = project_rows(residual_f, query_weight, key_weight, value_weight)
    running_max = jnp.full((f_dev, HEADS, CELLS), -1e30, jnp.float32)
    panel_keys = lax.all_gather(key_rows, "frame", axis=0, tiled=True)
    panel_values = lax.all_gather(value_rows, "frame", axis=0, tiled=True)
    count_keys = panel_keys.shape[0]
    scores = jnp.einsum(
        "qhdc,khdc->qkhc", queries, panel_keys, preferred_element_type=jnp.float32
    ) * HD ** (-0.5)
    key_mask = (jnp.arange(count_keys) < length)[None, :, None, None]
    scores = jnp.where(key_mask, scores, -1e30)
    new_max = jnp.maximum(running_max, jnp.max(scores, axis=1))
    raw_weights = jnp.where(key_mask, jnp.exp(scores - new_max[:, None]), 0.0)
    new_sum = jnp.sum(raw_weights, axis=1)
    addition = jnp.einsum(
        "qkhc,khdc->qhdc",
        raw_weights.astype(jnp.bfloat16),
        panel_values,
        preferred_element_type=jnp.float32,
    )
    attended = (addition / new_sum[:, :, None, :]).astype(jnp.bfloat16)
    encoded = finish_rows(residual_f, attended, out_weight, valid_rows)
    squares = jnp.sum(jnp.square(encoded.astype(jnp.float32)))
    grand_total = lax.psum(squares, ("scene", "frame"))
    slot_count = float(lax.axis_size("scene") * lax.axis_size("frame") * f_dev * CELLS * C2)
    kl_loss = 0.5 * grand_total / slot_count
    return (encoded[None], kl_loss)


def solution(mesh):
    placed = (P("scene", "frame", None, None), P("scene"), P(), P(), P(), P(), P(), P(), P())
    return jax.shard_map(
        shards,
        mesh=mesh,
        in_specs=placed,
        out_specs=(P("scene", "frame", None, None), P()),
        check_vma=False,
    )
```

profile of v0, /device:TPU:1, one launch (start us, length us, event | category | flops | bytes accessed | tf_op | source)
XLA Modules:
  0.0 420.5 jit_solution(17460069256639030074)
XLA Ops:
  7.9 2.6 copy.62
  10.6 2.9 reshape.49
  13.4 1.1 copy.59
  14.5 1.5 reshape.48
  16.0 5.0 %fusion.28 = bf16[4,128,8,8,8]{1,0,4,3,2:T(4,128)(2,1)S(1)} fusion(bf16[4,64,16,16,8]{1,4,3,2,0:T(8,128)(2,1)S(1)} %bitcast.90, bf16[128,64,3,3,3]{0,4,3,2,1:T(4,128)(2,1)S(1)} %reshape.48), kind=kOutput, calls=%fused_computation.44 | convolution fusion | flops 764018688 | bytes 2015232 | tf_op jit(solution)/shard_map/conv_general_dilated | solution.py:39
  21.0 7.9 %multiply_convert_fusion = (bf16[4,256,8,8,8]{1,0,4,3,2:T(4,128)(2,1)S(1)}, f32[4,256,8,8,8]{1,0,4,3,2:T(4,128)}) fusion(f32[4]{0:T(128)S(1)} %compare_convert_fusion, bf16[4,128,8,8,8]{1,0,4,3,2:T(4,128)(2,1)S(1)} %fusion.28, bf16[256,128,3,3,3]{0,4,3,2,1:T(4,128)(2,1)S(1)} %copy-done.1), kind=kOutput, calls=%fused_computation.24 | convolution fusion | flops 2794455040 | bytes 5439504 | tf_op jit(solution)/shard_map/conv_general_dilated | solution.py:39
  28.9 1.9 copy.64
  30.8 0.3 multiply_convert_fusion.1
  31.2 4.0 collective-permute-start
  35.1 1.5 collective-permute-start.1
  36.6 0.5 fusion.26
  37.1 3.0 collective-permute-done
  40.1 0.4 fusion.24
  40.5 3.4 collective-permute-done.1
  43.9 1.1 fusion.2
  45.0 1.4 convolution_convert_fusion.1
  46.5 1.4 convolution_convert_fusion.2
  48.0 0.5 convolution_convert_fusion
  48.4 2.5 copy.67
  50.9 112.4 %all-gather.5.cloned.1.call-done = bf16[64,4,64,512]{3,2,1,0:T(8,128)(2,1)} async-done(((bf16[4,4,64,512]{3,2,1,0:T(8,128)(2,1)}), bf16[64,4,64,512]{3,2,1,0:T(8,128)(2,1)}) %all-gather.5.cloned.1.call-update) | async-done | bytes 16777232 | tf_op jit(solution)/shard_map/all_gather | solution.py:125
  163.3 46.8 %copy.66 = bf16[64,4,64,512]{2,0,3,1:T(8,128)(2,1)} copy(bf16[64,4,64,512]{3,2,1,0:T(8,128)(2,1)} %all-gather.5.cloned.1.call-done) | data formatting | bytes 33554432 | tf_op jit(solution)/shard_map/all_gather | solution.py:125
  210.1 24.4 %bitcast_reduce_fusion = (f32[4,4,512]{0,2,1:T(8,128)}, f32[4,512,64,4]{2,3,1,0:T(4,128)}) fusion(pred[64]{0:T(512)(128)(4,1)S(1)} %iota_compare_fusion, bf16[64,4,64,512]{2,0,3,1:T(8,128)(2,1)} %copy.66, bf16[4,4,64,512]{2,0,3,1:T(4,128)(2,1)S(1)} %copy-done.2), kind=kOutput, calls=%fused_computation.1 | convolution fusion | flops 68673536 | bytes 19955776 | tf_op jit(solution)/shard_map/qhdc,khdc->qkhc/dot_general | solution.py:128
  234.5 1.4 broadcast_maximum_fusion
  235.9 30.0 %fusion.20 = f32[4,4,512]{0,2,1:T(8,128)S(1)} fusion(f32[4,4,512]{0,2,1:T(8,128)S(1)} %broadcast_maximum_fusion, f32[4,512,64,4]{2,3,1,0:T(4,128)} %get-tuple-element.9, pred[64]{0:T(512)(128)(4,1)S(1)} %iota_compare_fusion), kind=kLoop, calls=%fused_computation.34 | loop fusion | flops 2613248 | bytes 2162752 | tf_op jit(solution)/shard_map/reduce_sum | solution.py:135
  265.9 0.3 copy.70
  266.2 10.9 %all-gather.3.cloned.1.call-done = bf16[64,4,64,512]{3,2,1,0:T(8,128)(2,1)} async-done(((bf16[4,4,64,512]{3,2,1,0:T(8,128)(2,1)}), bf16[64,4,64,512]{3,2,1,0:T(8,128)(2,1)}) %all-gather.3.cloned.1.call-update) | async-done | bytes 16777232 | tf_op jit(solution)/shard_map/all_gather | solution.py:126
  277.1 46.6 %copy.68 = bf16[64,4,64,512]{2,0,3,1:T(8,128)(2,1)} copy(bf16[64,4,64,512]{3,2,1,0:T(8,128)(2,1)} %all-gather.3.cloned.1.call-done) | data formatting | bytes 33554432 | tf_op jit(solution)/shard_map/all_gather | solution.py:126
  323.7 17.5 %fusion.11 = f32[4,512,64,4]{2,3,1,0:T(4,128)} fusion(bf16[64,4,64,512]{2,0,3,1:T(8,128)(2,1)} %copy.68, f32[4,512,64,4]{2,3,1,0:T(4,128)} %get-tuple-element.9, f32[4,4,512]{0,2,1:T(8,128)S(1)} %broadcast_maximum_fusion, pred[64]{0:T(512)(128)(4,1)S(1)} %iota_compare_fusion), kind=kOutput, calls=%fused_computation.22 | convolution fusion | flops 69730304 | bytes 21004352 | tf_op jit(solution)/shard_map/qkhc,khdc->qhdc/dot_general | solution.py:136
  341.2 3.5 copy.69
  344.7 0.3 fusion.6
  345.0 2.3 multiply_reduce_fusion
  347.3 64.6 %psum.7 = f32[]{:T(128)} all-reduce(f32[]{:T(128)} %get-tuple-element.10), channel_id=1, replica_groups=mesh['scene'=8,'frame'=16] {'scene','frame'}, use_global_device_ids=true, to_apply=%region_4.5 | all-reduce | flops 1 | bytes 8 | tf_op jit(solution)/shard_map/psum | solution.py:145
  (24 shorter events, 0.2 us)
Async XLA Ops:
  7.2 337.9 %copy-start = (bf16[256,256]{1,0:T(8,128)(2,1)S(1)}, bf16[256,256]{1,0:T(8,128)(2,1)}, u32[]{:S(2)}) copy-start(bf16[256,256]{1,0:T(8,128)(2,1)} %param.17) | copy-start | bytes 393220
  7.2 156.1 %all-gather.5.cloned.1.call-start = ((), (), s32[]{:S(2)}) async-start(), calls=%async_computation.1 | async-start | bytes 17825792 | tf_op jit(solution)/shard_map/all_gather | solution.py:125
  10.5 2.9 copy-start.3
  16.0 5.0 %copy-start.1 = (bf16[256,128,3,3,3]{0,4,3,2,1:T(4,128)(2,1)S(1)}, bf16[256,128,3,3,3]{0,4,3,2,1:T(4,128)(2,1)}, u32[]{:S(2)}) copy-start(bf16[256,128,3,3,3]{0,4,3,2,1:T(4,128)(2,1)} %reshape.49) | copy-start | bytes 5308420
  30.8 5.8 %copy-start.4 = (bf16[3,256,256]{2,1,0:T(8,128)(2,1)S(1)}, bf16[3,256,256]{2,1,0:T(8,128)(2,1)}, u32[]{:S(2)}) copy-start(bf16[3,256,256]{2,1,0:T(8,128)(2,1)} %param.13) | copy-start | bytes 1179652
  31.2 8.9 %collective-permute-start = (bf16[1,256,512]{2,1,0:T(8,128)(2,1)S(1)}, bf16[1,256,512]{2,1,0:T(8,128)(2,1)S(1)}, u32[]{:S(2)}, u32[]{:S(2)}) collective-permute-start(bf16[1,256,512]{2,1,0:T(8,128)(2,1)S(1)} %get-tuple-element.3), channel_id=1, source_target_pairs={{0,1},{1,2},{2,3},{3,4},{4,5},{5,6},{6,7},{7,8},{8,9},{9,10},{10,1... | collective-permute-start | bytes 786440 | tf_op jit(solution)/shard_map/ppermute | solution.py:27
  35.1 8.7 %collective-permute-start.1 = (bf16[1,256,512]{2,1,0:T(8,128)(2,1)S(1)}, bf16[1,256,512]{2,1,0:T(8,128)(2,1)S(1)}, u32[]{:S(2)}, u32[]{:S(2)}) collective-permute-start(bf16[1,256,512]{2,1,0:T(8,128)(2,1)S(1)} %get-tuple-element.2), channel_id=1, source_target_pairs={{1,0},{2,1},{3,2},{4,3},{5,4},{6,5},{7,6},{8,7},{9,8},{10,9},{11,1... | collective-permute-start | bytes 786440 | tf_op jit(solution)/shard_map/ppermute | solution.py:29
  40.5 4.5 %copy-start.5 = (bf16[256,256]{1,0:T(8,128)(2,1)S(1)}, bf16[256,256]{1,0:T(8,128)(2,1)}, u32[]{:S(2)}) copy-start(bf16[256,256]{1,0:T(8,128)(2,1)} %param.15) | copy-start | bytes 393220
  44.9 1.5 copy-start.6
  46.4 1.6 copy-start.7
  46.4 230.7 %all-gather.3.cloned.1.call-start = ((), (), s32[]{:S(2)}) async-start(), calls=%async_computation | async-start | bytes 17825792 | tf_op jit(solution)/shard_map/all_gather | solution.py:126
  50.9 159.2 %copy-start.2 = (bf16[4,4,64,512]{2,0,3,1:T(4,128)(2,1)S(1)}, bf16[4,4,64,512]{2,0,3,1:T(4,128)(2,1)}, u32[]{:S(2)}) copy-start(bf16[4,4,64,512]{2,0,3,1:T(4,128)(2,1)} %copy.67) | copy-start | bytes 3145732
Sparse Core Ops, SparseCore 0:
  46.6 116.7 all-gather.4
  166.0 111.0 all-gather.2
where the time goes:
time: 423 us; the launch traced here: 421 us
  waiting for transfers between devices  130 us (31%)
  local copies, waits for them, and re-layouts  110 us (26%)
  blocking collectives  64.6 us (15%)
  matrix products  62.2 us (15%)
  other arithmetic  32 us (8%)
  between operations  16.7 us (4%)
  starting transfers between devices  5.51 us (1%)
    all_gather x1, waiting for transfers between devices, shards(): panel_keys = lax.all_gather(key_rows, 'frame', axis=0, tiled=True)  112 us
    psum x1, blocking collectives, shards(): grand_total = lax.psum(squares, ('scene', 'frame'))  64.6 us
    all_gather x1, local copies, waits for them, and re-layouts, shards(): panel_keys = lax.all_gather(key_rows, 'frame', axis=0, tiled=True)  46.8 us
    all_gather x1, local copies, waits for them, and re-layouts, shards(): panel_values = lax.all_gather(value_rows, 'frame', axis=0, tiled=True)  46.6 us
    reduce_sum x1, other arithmetic, shards(): new_sum = jnp.sum(raw_weights, axis=1)  30 us
    dot_general x1, matrix products, shards(): jnp.einsum('qhdc,khdc->qkhc', queries, panel_keys, preferred_element_type...  24.4 us
    dot_general x1, matrix products, shards(): jnp.einsum('qkhc,khdc->qhdc', raw_weights.astype(jnp.bfloat16), panel_val...  17.5 us
    conv_general_dilated x2, matrix products, spatial_conv(): lax.conv_general_dilated(voxels, kernel, (stride, stride, 1), ((1, 1), (1...  12.8 us
  transfers between devices with their start and end apart: 4, of which 4 were waited for; matrix products, arithmetic and copies ran while one was open for 26% of the time, Pallas kernels for 0%

commit v1 on v0

v1 whole, which is shorter than its diff:
```python
import jax
import jax.numpy as jnp
from jax import lax
from jax.sharding import PartitionSpec as P

CIN = 64
C1 = 128
C2 = 256
HEADS = 4
HD = 64
HI = 16
ZD = 8
CELLS = 512


NORM_EPS = 1e-06


def spatial_conv(voxels, weight, channels_in, stride):
    channels_out = weight.shape[0]
    kernel = weight.reshape(channels_out, channels_in, 3, 3, 3)
    return lax.conv_general_dilated(
        voxels,
        kernel,
        (stride, stride, 1),
        ((1, 1), (1, 1), (1, 1)),
        dimension_numbers=("NCDHW", "OIDHW", "NCDHW"),
        preferred_element_type=jnp.float32,
    )


def mix(maps, weight):
    return jnp.einsum("tnc,oc->tno", maps, weight, preferred_element_type=jnp.float32)


def shards(
    occupancy,
    scene_lengths,
    conv1_weight,
    conv2_weight,
    temporal_weight,
    query_weight,
    key_weight,
    value_weight,
    out_weight,
):
    f_dev = occupancy.shape[1]
    length = scene_lengths[0]
    first_frame = lax.axis_index("frame") * f_dev
    frame_ids = first_frame + jnp.arange(f_dev, dtype=jnp.int32)
    valid_rows = (frame_ids < length).astype(jnp.float32)
    voxels = occupancy[0].reshape(f_dev, CIN, HI, HI, ZD)
    first_maps = jax.nn.silu(spatial_conv(voxels, conv1_weight, CIN, 2)).astype(jnp.bfloat16)
    second_full = jax.nn.silu(spatial_conv(first_maps, conv2_weight, C1, 1))
    second_maps = (second_full.reshape(f_dev, C2, CELLS) * valid_rows[:, None, None]).astype(
        jnp.bfloat16
    )
    second = lax.all_to_all(second_maps.transpose(0, 2, 1), "frame", 1, 0, tiled=True)
    frames, cells = second.shape[:2]
    padded = jnp.pad(second, ((1, 1), (0, 0), (0, 0)))
    temporal_sum = mix(padded[0:frames], temporal_weight[0])
    for tap in range(1, 3):
        temporal_sum = temporal_sum + mix(padded[tap : tap + frames], temporal_weight[tap])
    residual = (second.astype(jnp.float32) + jax.nn.silu(temporal_sum)).astype(jnp.bfloat16)
    residual = residual.astype(jnp.float32)
    normed = (
        residual * lax.rsqrt(jnp.mean(residual * residual, axis=2, keepdims=True) + NORM_EPS)
    ).astype(jnp.bfloat16)
    split = (frames, cells, HEADS, HD)
    queries = mix(normed, query_weight).astype(jnp.bfloat16).reshape(split)
    keys = mix(normed, key_weight).astype(jnp.bfloat16).reshape(split)
    values = mix(normed, value_weight).astype(jnp.bfloat16).reshape(split)
    scores = jnp.einsum(
        "qnhd,knhd->nhqk", queries, keys, preferred_element_type=jnp.float32
    ) * HD ** (-0.5)
    key_mask = (jnp.arange(frames) < length)[None, None, None, :]
    scores = jnp.where(key_mask, scores, -1e30)
    row_max = jnp.max(scores, axis=3, keepdims=True)
    weights = jnp.where(key_mask, jnp.exp(scores - row_max), 0.0)
    total = jnp.sum(weights, axis=3, keepdims=True)
    weighted = jnp.einsum(
        "nhqk,knhd->nhqd",
        weights.astype(jnp.bfloat16),
        values,
        preferred_element_type=jnp.float32,
    )
    attended = (weighted / total).astype(jnp.bfloat16)
    attended = attended.transpose(2, 0, 1, 3).reshape(frames, cells, C2)
    row_valid = (jnp.arange(frames) < length).astype(jnp.float32)[:, None, None]
    encoded = ((residual + mix(attended, out_weight)) * row_valid).astype(jnp.bfloat16)
    squares = jnp.sum(jnp.square(encoded.astype(jnp.float32)))
    grand_total = lax.psum(squares, ("scene", "frame"))
    slot_count = float(lax.axis_size("scene") * frames * CELLS * C2)
    kl_loss = 0.5 * grand_total / slot_count
    encoded = lax.all_to_all(encoded, "frame", 0, 1, tiled=True).transpose(0, 2, 1)
    return (encoded[None], kl_loss)


def solution(mesh):
    placed = (P("scene", "frame", None, None), P("scene"), P(), P(), P(), P(), P(), P(), P())
    return jax.shard_map(
        shards,
        mesh=mesh,
        in_specs=placed,
        out_specs=(P("scene", "frame", None, None), P()),
        check_vma=False,
    )
```

time: 423 us -> 163 us (0.39)
  waiting for transfers between devices: 130 us -> 16 us
  local copies, waits for them, and re-layouts: 110 us -> 25.7 us
  matrix products: 62.2 us -> 28.9 us
  other arithmetic: 32 us -> 3.44 us
  between operations: 16.7 us -> 3.32 us
  blocking collectives: 64.6 us -> 72.7 us
  starting transfers between devices: 5.51 us -> 12.8 us
    all_gather x2 -> x0, waiting for transfers between devices: 123 us -> none  [the longest x1 112 us: shards(): panel_keys = lax.all_gather(key_rows, 'frame', axis=0, tiled=True)]
    all_gather x2 -> x0, local copies, waits for them, and re-layouts: 93.4 us -> none  [the longest x1 46.8 us: shards(): panel_keys = lax.all_gather(key_rows, 'frame', axis=0, tiled=True)]
    dot_general x9, matrix products: 49.4 us -> 17.3 us  [the longest x7 9.93 us: mix(): jnp.einsum('tnc,oc->tno', maps, weight, preferred_element_type=jnp.float32)]
    reduce_sum x1 -> x0, other arithmetic: 30 us -> none  [shards(): new_sum = jnp.sum(raw_weights, axis=1)]
    all_to_all x0 -> x2, waiting for transfers between devices: none -> 16 us  [the longest x1 16 us: shards(): lax.all_to_all(second_maps.transpose(0, 2, 1), 'frame', 1, 0, tiled=True)]
    all_to_all x0 -> x2, starting transfers between devices: none -> 12.8 us  [the longest x1 8.57 us: shards(): lax.all_to_all(second_maps.transpose(0, 2, 1), 'frame', 1, 0, tiled=True)]
    reshape x2 -> x4, local copies, waits for them, and re-layouts: 4.42 us -> 14.4 us  [the longest x1 4.45 us: shards(): keys = mix(normed, key_weight).astype(jnp.bfloat16).reshape(split)]
    psum x1, blocking collectives: 64.6 us -> 72.7 us  [shards(): grand_total = lax.psum(squares, ('scene', 'frame'))]
  transfers between devices with their start and end apart: 4 -> 2, of which waited for: 4 -> 1; matrix products, arithmetic and copies ran while one was open for 26% -> 0% of each run, Pallas kernels for 0% -> 0%
where the time goes in v1:
time: 163 us
  blocking collectives  72.7 us (45%)
  matrix products  28.9 us (18%)
  local copies, waits for them, and re-layouts  25.7 us (16%)
  waiting for transfers between devices  16 us (10%)
  starting transfers between devices  12.8 us (8%)
  other arithmetic  3.44 us (2%)
  between operations  3.32 us (2%)
    psum x1, blocking collectives, shards(): grand_total = lax.psum(squares, ('scene', 'frame'))  72.7 us
    all_to_all x1, waiting for transfers between devices, shards(): lax.all_to_all(second_maps.transpose(0, 2, 1), 'frame', 1, 0, tiled=True)  16 us
    conv_general_dilated x2, matrix products, spatial_conv(): lax.conv_general_dilated(voxels, kernel, (stride, stride, 1), ((1, 1), (1...  11.6 us
    dot_general x7, matrix products, mix(): jnp.einsum('tnc,oc->tno', maps, weight, preferred_element_type=jnp.float32)  9.93 us
    all_to_all x1, starting transfers between devices, shards(): lax.all_to_all(second_maps.transpose(0, 2, 1), 'frame', 1, 0, tiled=True)  8.57 us
    unnamed x19, local copies, waits for them, and re-layouts  5.05 us
    reshape x1, local copies, waits for them, and re-layouts, shards(): keys = mix(normed, key_weight).astype(jnp.bfloat16).reshape(split)  4.45 us
    reshape x1, local copies, waits for them, and re-layouts, shards(): values = mix(normed, value_weight).astype(jnp.bfloat16).reshape(split)  4.44 us
  transfers between devices with their start and end apart: 2, of which 1 were waited for; matrix products, arithmetic and copies ran while one was open for 0% of the time, Pallas kernels for 0%

profile of v1, /device:TPU:1, one launch (start us, length us, event | category | flops | bytes accessed | tf_op | source)
XLA Modules:
  0.0 162.8 jit_solution(13435538620634952501)
XLA Ops:
  0.6 0.0 copy-start
  1.3 2.6 %copy.23 = bf16[256,3456]{0,1:T(8,128)(2,1)S(1)} copy(bf16[256,3456]{1,0:T(8,128)(2,1)} %param.12) | data formatting | bytes 3538944 | tf_op args[3]
  4.0 0.0 copy-start.3
  4.0 2.9 %reshape.51 = bf16[256,128,3,3,3]{0,4,3,2,1:T(4,128)(2,1)} reshape(bf16[256,3456]{0,1:T(8,128)(2,1)S(1)} %copy.23) | data formatting | bytes 3538944 | tf_op jit(solution)/shard_map/reshape | solution.py:21
  6.8 1.1 copy.20
  7.9 1.5 reshape.50
  9.4 5.0 %fusion.22 = bf16[4,128,8,8,8]{1,0,4,3,2:T(4,128)(2,1)S(1)} fusion(bf16[4,64,16,16,8]{1,4,3,2,0:T(8,128)(2,1)S(1)} %bitcast.70, bf16[128,64,3,3,3]{0,4,3,2,1:T(4,128)(2,1)S(1)} %reshape.50), kind=kOutput, calls=%fused_computation.34 | convolution fusion | flops 764018688 | bytes 2015232 | tf_op jit(solution)/shard_map/conv_general_dilated | solution.py:22
  14.4 6.6 %divide_multiply_fusion = f32[4,256,8,8,8]{1,0,4,3,2:T(4,128)S(1)} fusion(bf16[4,128,8,8,8]{1,0,4,3,2:T(4,128)(2,1)S(1)} %fusion.22, bf16[256,128,3,3,3]{0,4,3,2,1:T(4,128)(2,1)S(1)} %copy-done.1), kind=kOutput, calls=%fused_computation.9 | convolution fusion | flops 2793406464 | bytes 4390912 | tf_op jit(solution)/shard_map/conv_general_dilated | solution.py:22
  21.0 1.5 fusion.7
  22.6 8.6 %all-to-all-start = ((bf16[4,512,256]{2,0,1:T(4,128)(2,1)}), bf16[4,512,256]{2,0,1:T(4,128)(2,1)S(1)}, u32[]{:S(2)}, u32[]{:S(2)}) async-start(bf16[4,512,256]{2,0,1:T(4,128)(2,1)} %bitcast.3), calls=%async_computation | async-start | bytes 2097152 | tf_op jit(solution)/shard_map/all_to_all | solution.py:58
  31.2 16.0 %all-to-all-done = bf16[4,512,256]{2,0,1:T(4,128)(2,1)S(1)} async-done(((bf16[4,512,256]{2,0,1:T(4,128)(2,1)}), bf16[4,512,256]{2,0,1:T(4,128)(2,1)S(1)}, u32[]{:S(2)}, u32[]{:S(2)}) %all-to-all-start) | async-done | bytes 1048608 | tf_op jit(solution)/shard_map/all_to_all | solution.py:58
  47.1 0.2 copy.25
  47.3 0.5 fusion.34
  47.8 0.5 fusion.36
  48.3 0.0 copy-start.5
  48.3 1.1 fusion.3
  49.5 1.5 convolution_convert_fusion.2
  50.9 3.4 %reshape.53 = bf16[64,32,4,64]{3,2,1,0:T(4,128)(2,1)S(1)} reshape(bf16[64,32,256]{2,1,0:T(8,128)(2,1)} %convolution_convert_fusion.2) | data formatting | bytes 2097152 | tf_op jit(solution)/shard_map/reshape | solution.py:70
  54.3 1.5 convolution_convert_fusion.1
  55.8 4.5 %reshape.54 = bf16[64,32,4,64]{3,2,1,0:T(4,128)(2,1)} reshape(bf16[64,32,256]{2,1,0:T(8,128)(2,1)} %convolution_convert_fusion.1) | data formatting | bytes 2097152 | tf_op jit(solution)/shard_map/reshape | solution.py:71
  60.2 1.5 convolution_convert_fusion
  61.7 4.4 %reshape.55 = bf16[64,32,4,64]{3,2,1,0:T(4,128)(2,1)} reshape(bf16[64,32,256]{2,1,0:T(8,128)(2,1)} %convolution_convert_fusion) | data formatting | bytes 2097152 | tf_op jit(solution)/shard_map/reshape | solution.py:72
  66.1 4.1 %fusion.9 = f32[32,4,64,64]{2,3,1,0:T(8,128)S(1)} fusion(bf16[64,32,4,64]{3,2,1,0:T(4,128)(2,1)} %reshape.54, bf16[64,32,4,64]{3,2,1,0:T(4,128)(2,1)S(1)} %reshape.53), kind=kOutput, calls=%fused_computation.17 | convolution fusion | flops 67108864 | bytes 4194304 | tf_op jit(solution)/shard_map/qnhd,knhd->nhqk/dot_general | solution.py:73
  70.3 1.9 %fusion.44 = (f32[32,4,64]{2,1,0:T(4,128)S(1)}, bf16[32,4,64,64]{2,3,1,0:T(8,128)(2,1)S(1)}) fusion(f32[32,4,64,64]{2,3,1,0:T(8,128)S(1)} %fusion.9, pred[64]{0:T(512)(128)(4,1)S(1)} %get-tuple-element.10), kind=kOutput, calls=%fused_computation.54 | output fusion | flops 4194367 | bytes 3178560 | tf_op jit(solution)/shard_map/sub | solution.py:79
  72.2 3.3 %fusion.1 = bf16[64,32,4,64]{3,0,2,1:T(8,128)(2,1)S(1)} fusion(bf16[64,32,4,64]{3,2,1,0:T(4,128)(2,1)S(1)} %copy-done.2, f32[64,32,4]{0,2,1:T(4,128)S(1)} %bitcast.71, bf16[32,4,64,64]{2,3,1,0:T(8,128)(2,1)S(1)} %get-tuple-element.7), kind=kOutput, calls=%fused_computation.2 | convolution fusion | flops 68157440 | bytes 3178496 | tf_op jit(solution)/shard_map/nhqk,knhd->nhqd/dot_general | solution.py:81
  75.4 1.6 copy.30
  77.1 2.2 %reshape.56 = bf16[64,32,256]{2,1,0:T(8,128)(2,1)} reshape(bf16[64,32,4,64]{3,2,1,0:T(4,128)(2,1)S(1)} %copy.30) | data formatting | bytes 2097152 | tf_op jit(solution)/shard_map/reshape | solution.py:88
  79.2 3.5 %multiply_reduce_fusion = (f32[]{:T(128)}, bf16[64,32,256]{2,1,0:T(8,128)(2,1)}) fusion(f32[64]{0:T(128)S(1)} %get-tuple-element.11, bf16[64,32,256]{2,1,0:T(8,128)(2,1)} %reshape.56, bf16[256,256]{1,0:T(8,128)(2,1)S(1)} %copy-done, bf16[64,32,256]{2,1,0:T(8,128)(2,1)S(1)} %get-tuple-element.5), kind=kOutput, calls=%fused_computation.20 | convolution fusion | flops 272105472 | bytes 3277060 | tf_op jit(solution)/shard_map/tnc,oc->tno/dot_general | solution.py:33
  82.7 4.2 %all-to-all-start.1 = ((bf16[64,32,256]{2,1,0:T(8,128)(2,1)}), bf16[64,32,256]{2,1,0:T(8,128)(2,1)S(1)}, u32[]{:S(2)}, u32[]{:S(2)}) async-start(bf16[64,32,256]{2,1,0:T(8,128)(2,1)} %get-tuple-element.9), calls=%async_computation.1 | async-start | bytes 2097152 | tf_op jit(solution)/shard_map/all_to_all | solution.py:95
  86.9 72.7 %psum.7 = f32[]{:T(128)} all-reduce(f32[]{:T(128)} %get-tuple-element.8), channel_id=1, replica_groups=mesh['scene'=8,'frame'=16] {'scene','frame'}, use_global_device_ids=true, to_apply=%region_4.5 | all-reduce | flops 1 | bytes 8 | tf_op jit(solution)/shard_map/psum | solution.py:92
  160.2 0.1 copy.31
  160.3 1.3 copy.32
  (17 shorter events, 0.1 us)
Async XLA Ops:
  0.6 78.6 %copy-start = (bf16[256,256]{1,0:T(8,128)(2,1)S(1)}, bf16[256,256]{1,0:T(8,128)(2,1)}, u32[]{:S(2)}) copy-start(bf16[256,256]{1,0:T(8,128)(2,1)} %param.17) | copy-start | bytes 393220
  4.0 2.9 %copy-start.3 = (bf16[1,4,64,2048]{3,2,1,0:T(8,128)(2,1)S(1)}, bf16[1,4,64,2048]{3,2,1,0:T(8,128)(2,1)}, u32[]{:S(2)}) copy-start(bf16[1,4,64,2048]{3,2,1,0:T(8,128)(2,1)} %param.9) | copy-start | bytes 3145732
  9.4 5.0 %copy-start.1 = (bf16[256,128,3,3,3]{0,4,3,2,1:T(4,128)(2,1)S(1)}, bf16[256,128,3,3,3]{0,4,3,2,1:T(4,128)(2,1)}, u32[]{:S(2)}) copy-start(bf16[256,128,3,3,3]{0,4,3,2,1:T(4,128)(2,1)} %reshape.51) | copy-start | bytes 5308420
  22.6 24.8 %copy-start.4 = (bf16[3,256,256]{2,1,0:T(8,128)(2,1)S(1)}, bf16[3,256,256]{2,1,0:T(8,128)(2,1)}, u32[]{:S(2)}) copy-start(bf16[3,256,256]{2,1,0:T(8,128)(2,1)} %param.13) | copy-start | bytes 1179652
  22.6 24.6 %all-to-all-start = ((bf16[4,512,256]{2,0,1:T(4,128)(2,1)}), bf16[4,512,256]{2,0,1:T(4,128)(2,1)S(1)}, u32[]{:S(2)}, u32[]{:S(2)}) async-start(bf16[4,512,256]{2,0,1:T(4,128)(2,1)} %bitcast.3), calls=%async_computation | async-start | bytes 2097152 | tf_op jit(solution)/shard_map/all_to_all | solution.py:58
  48.3 1.2 copy-start.5
  50.9 3.4 %copy-start.6 = (bf16[256,256]{1,0:T(8,128)(2,1)S(1)}, bf16[256,256]{1,0:T(8,128)(2,1)}, u32[]{:S(2)}) copy-start(bf16[256,256]{1,0:T(8,128)(2,1)} %param.15) | copy-start | bytes 393220
  55.8 4.5 %copy-start.7 = (bf16[256,256]{1,0:T(8,128)(2,1)S(1)}, bf16[256,256]{1,0:T(8,128)(2,1)}, u32[]{:S(2)}) copy-start(bf16[256,256]{1,0:T(8,128)(2,1)} %param.16) | copy-start | bytes 393220
  70.3 1.9 %copy-start.2 = (bf16[64,32,4,64]{3,2,1,0:T(4,128)(2,1)S(1)}, bf16[64,32,4,64]{3,2,1,0:T(4,128)(2,1)}, u32[]{:S(2)}) copy-start(bf16[64,32,4,64]{3,2,1,0:T(4,128)(2,1)} %reshape.55) | copy-start | bytes 3145732
  82.7 77.5 %all-to-all-start.1 = ((bf16[64,32,256]{2,1,0:T(8,128)(2,1)}), bf16[64,32,256]{2,1,0:T(8,128)(2,1)S(1)}, u32[]{:S(2)}, u32[]{:S(2)}) async-start(bf16[64,32,256]{2,1,0:T(8,128)(2,1)} %get-tuple-element.9), calls=%async_computation.1 | async-start | bytes 2097152 | tf_op jit(solution)/shard_map/all_to_all | solution.py:95

commit v2 on v1

v2 whole, which is shorter than its diff:
```python
import functools

import jax
import jax.numpy as jnp
from jax import lax
from jax.experimental import pallas as pl
from jax.experimental.pallas import tpu as pltpu
from jax.sharding import PartitionSpec as P

CIN = 64
C1 = 128
C2 = 256
HEADS = 4
HD = 64
HI = 16
ZD = 8
CELLS = 512


NORM_EPS = 1e-06


def spatial_conv(voxels, weight, channels_in, stride):
    channels_out = weight.shape[0]
    kernel = weight.reshape(channels_out, channels_in, 3, 3, 3)
    return lax.conv_general_dilated(
        voxels,
        kernel,
        (stride, stride, 1),
        ((1, 1), (1, 1), (1, 1)),
        dimension_numbers=("NCDHW", "OIDHW", "NCDHW"),
        preferred_element_type=jnp.float32,
    )


FRAMES = 64
CHUNKS = 2
LOG2_E = 1.4426950408889634


def by_rows(rows, weight):
    return lax.dot_general(
        rows, weight, (((1,), (1,)), ((), ())), preferred_element_type=jnp.float32
    )


def silu(v):
    return v / (1.0 + jnp.exp(-v))


def mixing_kernel(
    count,
    scenes,
    length_ref,
    second_ref,
    temporal_ref,
    query_ref,
    key_ref,
    value_ref,
    out_weight_ref,
    encoded_ref,
    loss_ref,
    gathered,
    residual,
    q_rows,
    k_rows,
    v_rows,
    att_rows,
    done_rows,
    returned,
    total,
    frame_sums,
    scene_sums,
    there_send,
    there_recv,
    back_send,
    back_recv,
    frame_send,
    frame_recv,
    scene_send,
    scene_recv,
):
    f_dev = second_ref.shape[0]
    cells = CELLS // count
    part = cells // CHUNKS
    rows = FRAMES * part
    me = lax.axis_index("frame")
    my_scene = lax.axis_index("scene")
    length = length_ref[0]

    barrier = pltpu.get_barrier_semaphore()

    def greet_frame(d, carry):
        pl.semaphore_signal(
            barrier,
            inc=1,
            device_id={"frame": lax.rem(me + d, count)},
            device_id_type=pl.DeviceIdType.MESH,
        )
        return carry

    def greet_scene(d, carry):
        pl.semaphore_signal(
            barrier,
            inc=1,
            device_id={"scene": lax.rem(my_scene + d, scenes)},
            device_id_type=pl.DeviceIdType.MESH,
        )
        return carry

    lax.fori_loop(1, count, greet_frame, 0)
    lax.fori_loop(1, scenes, greet_scene, 0)
    pl.semaphore_wait(barrier, count - 1 + scenes - 1)

    def cells_of(device, chunk):
        return pl.ds(pl.multiple_of(device * cells + chunk * part, part), part)

    def there(chunk, d):
        to = lax.rem(me + d, count)
        return pltpu.make_async_remote_copy(
            src_ref=second_ref.at[:, cells_of(to, chunk), :],
            dst_ref=gathered.at[chunk, pl.ds(1 + f_dev * me, f_dev)],
            send_sem=there_send.at[chunk, d],
            recv_sem=there_recv.at[chunk, d],
            device_id={"frame": to},
            device_id_type=pl.DeviceIdType.MESH,
        )

    def back(chunk, d):
        to = lax.rem(me + d, count)
        return pltpu.make_async_remote_copy(
            src_ref=done_rows.at[chunk, pl.ds(f_dev * to, f_dev)],
            dst_ref=returned.at[:, cells_of(me, chunk), :],
            send_sem=back_send.at[chunk, d],
            recv_sem=back_recv.at[chunk, d],
            device_id={"frame": to},
            device_id_type=pl.DeviceIdType.MESH,
        )

    def frame_sum(d):
        return pltpu.make_async_remote_copy(
            src_ref=total,
            dst_ref=frame_sums.at[me],
            send_sem=frame_send.at[d],
            recv_sem=frame_recv.at[d],
            device_id={"frame": lax.rem(me + d, count)},
            device_id_type=pl.DeviceIdType.MESH,
        )

    def scene_sum(d):
        return pltpu.make_async_remote_copy(
            src_ref=total,
            dst_ref=scene_sums.at[my_scene],
            send_sem=scene_send.at[d],
            recv_sem=scene_recv.at[d],
            device_id={"scene": lax.rem(my_scene + d, scenes)},
            device_id_type=pl.DeviceIdType.MESH,
        )

    def each(first, last, act):
        def step(d, carry):
            act(d)
            return carry

        lax.fori_loop(first, last, step, 0)

    for chunk in range(CHUNKS):
        each(1, count, lambda d, chunk=chunk: there(chunk, d).start())
    for chunk in range(CHUNKS):
        gathered[chunk, 0] = jnp.zeros((part, C2), jnp.bfloat16)
        gathered[chunk, FRAMES + 1] = jnp.zeros((part, C2), jnp.bfloat16)
        gathered[chunk, pl.ds(1 + f_dev * me, f_dev)] = second_ref[:, cells_of(me, chunk), :]

    span = 256 // part
    block = span * part
    head_of = lax.broadcasted_iota(jnp.int32, (FRAMES, C2), 1) // HD
    ones4 = (
        lax.broadcasted_iota(jnp.int32, (C2, C2), 0) // HD
        == lax.broadcasted_iota(jnp.int32, (C2, C2), 1) // HD
    ).astype(jnp.bfloat16)
    key_mask = lax.broadcasted_iota(jnp.int32, (FRAMES, C2), 1) % FRAMES < length
    low_half = lax.broadcasted_iota(jnp.int32, (FRAMES, 128), 1) < HD
    total[...] = jnp.zeros_like(total)

    for chunk in range(CHUNKS):
        each(1, count, lambda d, chunk=chunk: there(chunk, d).wait_recv())

        def project(b, carry, chunk=chunk):
            window = gathered[chunk, pl.ds(b * span, span + 2)].reshape((span + 2) * part, C2)
            temporal = by_rows(window[:block], temporal_ref[0])
            temporal = temporal + by_rows(window[part : part + block], temporal_ref[1])
            temporal = temporal + by_rows(window[2 * part :], temporal_ref[2])
            here = window[part : part + block].astype(jnp.float32)
            mixed = (here + silu(temporal)).astype(jnp.bfloat16)
            at = pl.ds(pl.multiple_of(b * block, block), block)
            residual[at, :] = mixed
            wide = mixed.astype(jnp.float32)
            scale = lax.rsqrt(jnp.mean(wide * wide, axis=1, keepdims=True) + NORM_EPS)
            normed = (wide * scale).astype(jnp.bfloat16)
            for weight_ref, into in ((query_ref, q_rows), (key_ref, k_rows), (value_ref, v_rows)):
                made = by_rows(normed, weight_ref[...])
                into[0, at, :] = made[:, :128]
                into[1, at, :] = made[:, 128:]
            return carry

        lax.fori_loop(0, FRAMES // span, project, 0)

        def cell_rows(ref, cell):
            at = pl.ds(cell, FRAMES, stride=part)
            return jnp.concatenate([ref[0, at, :], ref[1, at, :]], axis=1).astype(jnp.bfloat16)

        def spread(found):
            zero = jnp.zeros_like(found)
            return jnp.concatenate([jnp.where(head_of == h, found, zero) for h in range(HEADS)], 0)

        def attend(cell, carry):
            queries = cell_rows(q_rows, cell)
            keys = spread(cell_rows(k_rows, cell))
            values = spread(cell_rows(v_rows, cell))
            scores = jnp.where(key_mask, by_rows(queries, keys), -1e30)
            tops = []
            for half in range(2):
                piece = scores[:, half * 128 : half * 128 + 128]
                low = jnp.max(jnp.where(low_half, piece, -1e30), axis=1, keepdims=True)
                high = jnp.max(jnp.where(low_half, -1e30, piece), axis=1, keepdims=True)
                tops.append(jnp.where(low_half, low, high))
            top = jnp.concatenate(tops, axis=1)
            weights = jnp.exp2((scores - top) * (LOG2_E * HD**-0.5)).astype(jnp.bfloat16)
            weighted = jnp.dot(weights, values, preferred_element_type=jnp.float32)
            sums = jnp.dot(weights, ones4, preferred_element_type=jnp.float32)
            attended = weighted / sums
            at = pl.ds(cell, FRAMES, stride=part)
            att_rows[0, at, :] = attended[:, :128]
            att_rows[1, at, :] = attended[:, 128:]
            return carry

        lax.fori_loop(0, part, attend, 0)

        def finish(b, carry, chunk=chunk):
            at = pl.ds(pl.multiple_of(b * block, block), block)
            attended = jnp.concatenate([att_rows[0, at, :], att_rows[1, at, :]], axis=1)
            full = residual[at, :].astype(jnp.float32) + by_rows(
                attended.astype(jnp.bfloat16), out_weight_ref[...]
            )
            frame = b * span + lax.broadcasted_iota(jnp.int32, (block, C2), 0) // part
            kept = jnp.where(frame < length, full, 0.0).astype(jnp.bfloat16)
            done_rows[chunk, pl.ds(b * span, span)] = kept.reshape(span, part, C2)
            wide = kept.astype(jnp.float32)
            squares = jnp.sum((wide * wide).reshape(block // 8, 8, C2), axis=0)
            total[...] += squares[:, :128] + squares[:, 128:]
            return carry

        lax.fori_loop(0, FRAMES // span, finish, 0)
        each(1, count, lambda d, chunk=chunk: back(chunk, d).start())
        returned[:, cells_of(me, chunk), :] = done_rows[chunk, pl.ds(f_dev * me, f_dev)]

    each(1, count, lambda d: frame_sum(d).start())
    frame_sums[me] = total[...]
    each(1, count, lambda d: frame_sum(d).wait_recv())
    each(1, count, lambda d: frame_sum(d).wait_send())
    total[...] = jnp.sum(frame_sums[...], axis=0)
    each(1, scenes, lambda d: scene_sum(d).start())
    scene_sums[my_scene] = total[...]

    eye = (
        lax.broadcasted_iota(jnp.int32, (C2, C2), 0)
        == lax.broadcasted_iota(jnp.int32, (C2, C2), 1)
    ).astype(jnp.bfloat16)
    for chunk in range(CHUNKS):
        each(1, count, lambda d, chunk=chunk: back(chunk, d).wait_recv())

    def turn(f, carry):
        encoded_ref[f] = by_rows(eye, returned[f]).astype(jnp.bfloat16)
        return carry

    lax.fori_loop(0, f_dev, turn, 0)

    each(1, scenes, lambda d: scene_sum(d).wait_recv())
    loss_ref[...] = jnp.sum(scene_sums[...], axis=0)
    each(1, scenes, lambda d: scene_sum(d).wait_send())
    for chunk in range(CHUNKS):
        each(1, count, lambda d, chunk=chunk: there(chunk, d).wait_send())
        each(1, count, lambda d, chunk=chunk: back(chunk, d).wait_send())


def shards(
    occupancy,
    scene_lengths,
    conv1_weight,
    conv2_weight,
    temporal_weight,
    query_weight,
    key_weight,
    value_weight,
    out_weight,
):
    f_dev = occupancy.shape[1]
    length = scene_lengths[0]
    count, scenes = lax.axis_size("frame"), lax.axis_size("scene")
    first_frame = lax.axis_index("frame") * f_dev
    frame_ids = first_frame + jnp.arange(f_dev, dtype=jnp.int32)
    valid_rows = (frame_ids < length).astype(jnp.float32)
    voxels = occupancy[0].reshape(f_dev, CIN, HI, HI, ZD)
    first_maps = jax.nn.silu(spatial_conv(voxels, conv1_weight, CIN, 2)).astype(jnp.bfloat16)
    second_full = jax.nn.silu(spatial_conv(first_maps, conv2_weight, C1, 1))
    second_maps = (second_full.reshape(f_dev, C2, CELLS) * valid_rows[:, None, None]).astype(
        jnp.bfloat16
    )
    second = second_maps.transpose(0, 2, 1)

    part = CELLS // count // CHUNKS
    rows = FRAMES * part
    wide_rows = pltpu.VMEM((2, rows, 128), jnp.float32)
    in_vmem = pl.BlockSpec(memory_space=pltpu.VMEM)
    encoded, sums = pl.pallas_call(
        functools.partial(mixing_kernel, count, scenes),
        out_shape=(
            jax.ShapeDtypeStruct((f_dev, C2, CELLS), jnp.bfloat16),
            jax.ShapeDtypeStruct((8, 128), jnp.float32),
        ),
        in_specs=[pl.BlockSpec(memory_space=pltpu.SMEM)] + [in_vmem] * 6,
        out_specs=(in_vmem, in_vmem),
        scratch_shapes=[
            pltpu.VMEM((CHUNKS, FRAMES + 2, part, C2), jnp.bfloat16),
            pltpu.VMEM((rows, C2), jnp.bfloat16),
            wide_rows,
            wide_rows,
            wide_rows,
            wide_rows,
            pltpu.VMEM((CHUNKS, FRAMES, part, C2), jnp.bfloat16),
            pltpu.VMEM((f_dev, CELLS, C2), jnp.bfloat16),
            pltpu.VMEM((8, 128), jnp.float32),
            pltpu.VMEM((count, 8, 128), jnp.float32),
            pltpu.VMEM((scenes, 8, 128), jnp.float32),
        ]
        + [pltpu.SemaphoreType.DMA((CHUNKS, count))] * 4
        + [pltpu.SemaphoreType.DMA((count,))] * 2
        + [pltpu.SemaphoreType.DMA((scenes,))] * 2,
        compiler_params=pltpu.CompilerParams(
            collective_id=0, has_side_effects=True, vmem_limit_bytes=48 * 2**20
        ),
    )(scene_lengths, second, temporal_weight, query_weight, key_weight, value_weight, out_weight)
    slot_count = float(scenes * FRAMES * CELLS * C2)
    kl_loss = 0.5 * jnp.sum(sums) / slot_count
    return (encoded[None], kl_loss)


def solution(mesh):
    placed = (P("scene", "frame", None, None), P("scene"), P(), P(), P(), P(), P(), P(), P())
    return jax.shard_map(
        shards,
        mesh=mesh,
        in_specs=placed,
        out_specs=(P("scene", "frame", None, None), P()),
        check_vma=False,
    )
```

time: 163 us -> 89.6 us (0.55)
  blocking collectives: 72.7 us -> 0 us
  Pallas kernels: 0 us -> 56.7 us
  waiting for transfers between devices: 16 us -> 0 us
  local copies, waits for them, and re-layouts: 25.7 us -> 10.6 us
  matrix products: 28.9 us -> 15.8 us
  starting transfers between devices: 12.8 us -> 0 us
    psum x1 -> x0, blocking collectives: 72.7 us -> none  [shards(): grand_total = lax.psum(squares, ('scene', 'frame'))]
    pallas_call x0 -> x1, Pallas kernels: none -> 56.7 us  [shards(): pl.pallas_call(functools.partial(mixing_kernel, count, scenes), out_shape...]
    dot_general x9 -> x0, matrix products: 17.3 us -> none  [the longest x7 9.93 us: mix(): jnp.einsum('tnc,oc->tno', maps, weight, preferred_element_type=jnp.float32)]
    all_to_all x2 -> x0, waiting for transfers between devices: 16 us -> none  [the longest x1 16 us: shards(): lax.all_to_all(second_maps.transpose(0, 2, 1), 'frame', 1, 0, tiled=True)]
    reshape x4 -> x0, local copies, waits for them, and re-layouts: 14.4 us -> none  [the longest x1 4.45 us: shards(): keys = mix(normed, key_weight).astype(jnp.bfloat16).reshape(split)]
    all_to_all x2 -> x0, starting transfers between devices: 12.8 us -> none  [the longest x1 8.57 us: shards(): lax.all_to_all(second_maps.transpose(0, 2, 1), 'frame', 1, 0, tiled=True)]
    conv_general_dilated x2 -> x1, matrix products: 11.6 us -> 15.8 us  [spatial_conv(): lax.conv_general_dilated(voxels, kernel, (stride, stride, 1), ((1, 1), (1...]
    mul x0 -> x1, other arithmetic: none -> 2.14 us  [shards(): second_full = jax.nn.silu(spatial_conv(first_maps, conv2_weight, C1, 1))]
  transfers between devices with their start and end apart: 2 -> 0, of which waited for: 1 -> 0; matrix products, arithmetic and copies ran while one was open for 0% -> 0% of each run, Pallas kernels for 0% -> 0%
where the time goes in v2:
time: 89.6 us; the launch traced here: 89.2 us
  Pallas kernels  56.7 us (63%)
  matrix products  15.8 us (18%)
  local copies, waits for them, and re-layouts  10.6 us (12%)
  between operations  3.16 us (4%)
  other arithmetic  2.98 us (3%)
    pallas_call x1, Pallas kernels, shards(): pl.pallas_call(functools.partial(mixing_kernel, count, scenes), out_shape...  56.7 us
    conv_general_dilated x1, matrix products, spatial_conv(): lax.conv_general_dilated(voxels, kernel, (stride, stride, 1), ((1, 1), (1...  15.8 us
    unnamed x17, local copies, waits for them, and re-layouts  6.25 us
    reshape x2, local copies, waits for them, and re-layouts, spatial_conv(): kernel = weight.reshape(channels_out, channels_in, 3, 3, 3)  4.35 us
    mul x1, other arithmetic, shards(): second_full = jax.nn.silu(spatial_conv(first_maps, conv2_weight, C1, 1))  2.14 us

profile of v2, /device:TPU:1, one launch (start us, length us, event | category | flops | bytes accessed | tf_op | source)
XLA Modules:
  0.0 89.2 jit_solution(12971572424687503225)
XLA Ops:
  1.3 2.6 %copy.24 = bf16[256,3456]{0,1:T(8,128)(2,1)S(1)} copy(bf16[256,3456]{1,0:T(8,128)(2,1)} %param.12) | data formatting | bytes 3538944 | tf_op args[3]
  3.9 0.0 copy-start.6
  3.9 2.9 %reshape.20 = bf16[256,128,3,3,3]{0,4,3,2,1:T(4,128)(2,1)} reshape(bf16[256,3456]{0,1:T(8,128)(2,1)S(1)} %copy.24) | data formatting | bytes 3538944 | tf_op jit(solution)/shard_map/reshape | solution.py:25
  6.8 0.0 copy-done.6
  6.8 0.0 copy-start.5
  6.8 1.8 %copy.21 = bf16[1,4,64,2048]{2,3,1,0:T(8,128)(2,1)} copy(bf16[1,4,64,2048]{3,2,1,0:T(8,128)(2,1)S(1)} %copy-done.6) | data formatting | bytes 2097152 | tf_op args[0]
  8.6 1.5 %reshape.19 = bf16[128,64,3,3,3]{0,4,3,2,1:T(4,128)(2,1)S(1)} reshape(bf16[128,1728]{0,1:T(8,128)(2,1)} %param.11) | data formatting | bytes 884736 | tf_op jit(solution)/shard_map/reshape | solution.py:25
  10.0 0.0 copy-done.5
  10.1 15.8 %fusion.3 = f32[4,256,8,8,8]{1,0,4,3,2:T(4,128)} fusion(bf16[256,128,3,3,3]{0,4,3,2,1:T(4,128)(2,1)S(1)} %copy-done.5, bf16[4,64,16,16,8]{1,4,3,2,0:T(8,128)(2,1)} %bitcast.15, bf16[128,64,3,3,3]{0,4,3,2,1:T(4,128)(2,1)S(1)} %reshape.19), kind=kOutput, calls=%fused_computation.5 | convolution fusion | flops 3555328000 | bytes 5357568 | tf_op jit(solution)/shard_map/conv_general_dilated | solution.py:26
  25.8 2.1 %divide_multiply_fusion = f32[4,256,8,8,8]{1,4,3,2,0:T(8,128)S(1)} fusion(f32[4,256,8,8,8]{1,0,4,3,2:T(4,128)} %fusion.3), kind=kLoop, calls=%fused_computation.2 | loop fusion | flops 2097152 | bytes 4194304 | tf_op jit(solution)/shard_map/jit(silu)/mul | solution.py:305
  28.0 0.0 copy-start
  28.0 0.0 copy-start.1
  28.0 0.0 copy-start.2
  28.0 0.0 copy-start.3
  28.0 0.0 copy-start.4
  28.1 0.2 fusion
  28.3 0.7 copy-done
  29.0 0.0 copy-done.1
  29.0 0.1 copy-done.2
  29.1 0.0 copy-done.3
  29.1 0.0 copy-done.4
  29.2 56.7 %shard_map.104 = (bf16[4,256,512]{2,1,0:T(8,128)(2,1)S(1)}, f32[8,128]{1,0:T(8,128)S(1)}) custom-call(s32[1]{0:T(128)} %copy.42.length_ref, bf16[4,512,256]{2,1,0:T(8,128)(2,1)S(1)} %bitcast.13, bf16[3,256,256]{2,1,0:T(8,128)(2,1)S(1)} %copy-done, bf16[256,256]{1,0:T(8,128)(2,1)S(1)} %copy-done.1, bf16[256,256]{1,0:T(8,128)(2,1)S(1)} %copy-done.2, ...), custom_call_target="tpu_custom_call" | custom-call | tf_op jit(solution)/shard_map/pallas_call | solution.py:315
  85.9 0.6 reduce_sum.9
  87.1 1.0 %copy.43 = bf16[1,4,256,512]{3,2,1,0:T(8,128)(2,1)} copy(bf16[1,4,256,512]{3,2,1,0:T(8,128)(2,1)S(1)} %bitcast.14) | data formatting | bytes 2097152
  (1 shorter events, 0.0 us)
Async XLA Ops:
  3.9 2.9 %copy-start.6 = (bf16[1,4,64,2048]{3,2,1,0:T(8,128)(2,1)S(1)}, bf16[1,4,64,2048]{3,2,1,0:T(8,128)(2,1)}, u32[]{:S(2)}) copy-start(bf16[1,4,64,2048]{3,2,1,0:T(8,128)(2,1)} %param.9) | copy-start | bytes 3145732
  6.8 3.2 %copy-start.5 = (bf16[256,128,3,3,3]{0,4,3,2,1:T(4,128)(2,1)S(1)}, bf16[256,128,3,3,3]{0,4,3,2,1:T(4,128)(2,1)}, u32[]{:S(2)}) copy-start(bf16[256,128,3,3,3]{0,4,3,2,1:T(4,128)(2,1)} %reshape.20) | copy-start | bytes 5308420
  28.0 1.0 %copy-start = (bf16[3,256,256]{2,1,0:T(8,128)(2,1)S(1)}, bf16[3,256,256]{2,1,0:T(8,128)(2,1)}, u32[]{:S(2)}) copy-start(bf16[3,256,256]{2,1,0:T(8,128)(2,1)} %temporal_ref.1) | copy-start | bytes 1179652
  28.0 1.0 %copy-start.1 = (bf16[256,256]{1,0:T(8,128)(2,1)S(1)}, bf16[256,256]{1,0:T(8,128)(2,1)}, u32[]{:S(2)}) copy-start(bf16[256,256]{1,0:T(8,128)(2,1)} %query_ref.1) | copy-start | bytes 393220
  28.0 1.1 %copy-start.2 = (bf16[256,256]{1,0:T(8,128)(2,1)S(1)}, bf16[256,256]{1,0:T(8,128)(2,1)}, u32[]{:S(2)}) copy-start(bf16[256,256]{1,0:T(8,128)(2,1)} %key_ref.1) | copy-start | bytes 393220
  28.0 1.1 %copy-start.3 = (bf16[256,256]{1,0:T(8,128)(2,1)S(1)}, bf16[256,256]{1,0:T(8,128)(2,1)}, u32[]{:S(2)}) copy-start(bf16[256,256]{1,0:T(8,128)(2,1)} %value_ref.1) | copy-start | bytes 393220
  28.0 1.1 %copy-start.4 = (bf16[256,256]{1,0:T(8,128)(2,1)S(1)}, bf16[256,256]{1,0:T(8,128)(2,1)}, u32[]{:S(2)}) copy-start(bf16[256,256]{1,0:T(8,128)(2,1)} %out_weight_ref.1) | copy-start | bytes 393220

commit v3 on v2

--- a/solution.py
+++ b/solution.py
@@ -2,6 +2,7 @@
 
 import jax
 import jax.numpy as jnp
+import numpy as np
 from jax import lax
 from jax.experimental import pallas as pl
 from jax.experimental.pallas import tpu as pltpu
@@ -20,19 +21,6 @@
 NORM_EPS = 1e-06
 
 
-def spatial_conv(voxels, weight, channels_in, stride):
-    channels_out = weight.shape[0]
-    kernel = weight.reshape(channels_out, channels_in, 3, 3, 3)
-    return lax.conv_general_dilated(
-        voxels,
-        kernel,
-        (stride, stride, 1),
-        ((1, 1), (1, 1), (1, 1)),
-        dimension_numbers=("NCDHW", "OIDHW", "NCDHW"),
-        preferred_element_type=jnp.float32,
-    )
-
-
 FRAMES = 64
 CHUNKS = 2
 LOG2_E = 1.4426950408889634
@@ -44,15 +32,103 @@
     )
 
 
+def by_columns(rows, matrix):
+    return jnp.dot(rows, matrix, preferred_element_type=jnp.float32)
+
+
 def silu(v):
-    return v / (1.0 + jnp.exp(-v))
+    return 0.5 * v * (1.0 + jnp.tanh(0.5 * v))
+
+
+def picks_strided():
+    picks = np.zeros((5, 8, ZD, 2, HI, ZD), np.float32)
+    for tap in range(9):
+        for out_y in range(8):
+            for out_z in range(ZD):
+                y, z = 2 * out_y + tap // 3 - 1, out_z + tap % 3 - 1
+                if 0 <= y < HI and 0 <= z < ZD:
+                    picks[tap // 2, out_y, out_z, tap % 2, y, z] = 1
+    return picks.reshape(5 * 64, 2 * HI * ZD)
+
+
+def picks_near():
+    picks = np.zeros((9, 8, ZD, 8, ZD), np.float32)
+    for tap in range(9):
+        for out_y in range(8):
+            for out_z in range(ZD):
+                y, z = out_y + tap // 3 - 1, out_z + tap % 3 - 1
+                if 0 <= y < 8 and 0 <= z < ZD:
+                    picks[tap, out_y, out_z, y, z] = 1
+    return picks.reshape(9 * 64, 64)
+
+
+def order_weights(conv1_ref, conv2_ref, tall1, tall2, taps1, taps2):
+    eye = (
+        lax.broadcasted_iota(jnp.int32, (128, 128), 0)
+        == lax.broadcasted_iota(jnp.int32, (128, 128), 1)
+    ).astype(jnp.bfloat16)
+    tall1[...] = conv1_ref[...].astype(jnp.float32)
+    for at in range(0, C1 * 27, 128):
+        turned = by_rows(eye, conv2_ref[:, at : at + 128])
+        tall2[0, at : at + 128, :] = turned[:, :128]
+        tall2[1, at : at + 128, :] = turned[:, 128:]
+    for dx in range(3):
+        for tap in range(9):
+            at = pl.ds(dx * 9 + tap, CIN, stride=27)
+            taps1[dx, tap * CIN : (tap + 1) * CIN, :] = tall1[at, :].astype(jnp.bfloat16)
+            at = pl.ds(dx * 9 + tap, C1, stride=27)
+            taps2[dx, tap * C1 : (tap + 1) * C1, :] = jnp.concatenate(
+                [tall2[0, at, :], tall2[1, at, :]], axis=1
+            ).astype(jnp.bfloat16)
+        taps1[dx, 9 * CIN :, :] = jnp.zeros((CIN, C1), jnp.bfloat16)
+
+
+def convolve_pair(
+    pair, first_frame, length, occupancy_ref, picks1, picks2, taps1, taps2, even, odd, maps, near, second
+):
+    blank = jnp.zeros((CIN, 128), jnp.bfloat16)
+    for x in range(HI):
+        pieces = []
+        for f in range(2):
+            plane = occupancy_ref[2 * pair + f, :, x * 128 : (x + 1) * 128]
+            pieces.append(jnp.concatenate([plane, blank], axis=1))
+            pieces.append(jnp.concatenate([blank, plane], axis=1))
+        found = by_rows(picks1[...], jnp.concatenate(pieces, axis=0)).astype(jnp.bfloat16)
+        into, row = (even, x // 2) if x % 2 == 0 else (odd, x // 2 + 1)
+        for f in range(2):
+            for k in range(5):
+                into[f, row, :, k * 128 : (k + 1) * 128] = found[
+                    k * 64 : (k + 1) * 64, f * 128 : (f + 1) * 128
+                ]
+    for f in range(2):
+        total = by_columns(odd[f, 0:8].reshape(CELLS, 10 * CIN), taps1[0])
+        total = total + by_columns(even[f].reshape(CELLS, 10 * CIN), taps1[1])
+        total = total + by_columns(odd[f, 1:9].reshape(CELLS, 10 * CIN), taps1[2])
+        maps[:, f * C1 : (f + 1) * C1] = silu(total).astype(jnp.bfloat16)
+    for x in range(8):
+        found = by_columns(picks2[...], maps[x * 64 : (x + 1) * 64, :]).astype(jnp.bfloat16)
+        for f in range(2):
+            for k in range(9):
+                near[f, x + 1, :, k * C1 : (k + 1) * C1] = found[
+                    k * 64 : (k + 1) * 64, f * C1 : (f + 1) * C1
+                ]
+    for f in range(2):
+        total = by_columns(near[f, 0:8].reshape(CELLS, 9 * C1), taps2[0])
+        total = total + by_columns(near[f, 1:9].reshape(CELLS, 9 * C1), taps2[1])
+        total = total + by_columns(near[f, 2:10].reshape(CELLS, 9 * C1), taps2[2])
+        kept = jnp.where(first_frame + 2 * pair + f < length, silu(total), 0.0)
+        second[2 * pair + f] = kept.astype(jnp.bfloat16)
 
 
 def mixing_kernel(
     count,
     scenes,
     length_ref,
-    second_ref,
+    occupancy_ref,
+    conv1_ref,
+    conv2_ref,
+    picks1,
+    picks2,
     temporal_ref,
     query_ref,
     key_ref,
@@ -60,6 +136,15 @@
     out_weight_ref,
     encoded_ref,
     loss_ref,
+    tall1,
+    tall2,
+    taps1,
+    taps2,
+    even,
+    odd,
+    maps,
+    near,
+    second,
     gathered,
     residual,
     q_rows,
@@ -80,7 +165,8 @@
     scene_send,
     scene_recv,
 ):
-    f_dev = second_ref.shape[0]
+    f_dev = occupancy_ref.shape[0]
+    pairs = f_dev // 2
     cells = CELLS // count
     part = cells // CHUNKS
     rows = FRAMES * part
@@ -110,18 +196,17 @@
 
     lax.fori_loop(1, count, greet_frame, 0)
     lax.fori_loop(1, scenes, greet_scene, 0)
-    pl.semaphore_wait(barrier, count - 1 + scenes - 1)
 
     def cells_of(device, chunk):
         return pl.ds(pl.multiple_of(device * cells + chunk * part, part), part)
 
-    def there(chunk, d):
+    def there(chunk, pair, d):
         to = lax.rem(me + d, count)
         return pltpu.make_async_remote_copy(
-            src_ref=second_ref.at[:, cells_of(to, chunk), :],
-            dst_ref=gathered.at[chunk, pl.ds(1 + f_dev * me, f_dev)],
-            send_sem=there_send.at[chunk, d],
-            recv_sem=there_recv.at[chunk, d],
+            src_ref=second.at[pl.ds(2 * pair, 2), cells_of(to, chunk), :],
+            dst_ref=gathered.at[chunk, pl.ds(1 + f_dev * me + 2 * pair, 2)],
+            send_sem=there_send.at[chunk * pairs + pair, d],
+            recv_sem=there_recv.at[chunk * pairs + pair, d],
             device_id={"frame": to},
             device_id_type=pl.DeviceIdType.MESH,
         )
@@ -164,12 +249,36 @@
 
         lax.fori_loop(first, last, step, 0)
 
-    for chunk in range(CHUNKS):
-        each(1, count, lambda d, chunk=chunk: there(chunk, d).start())
+    order_weights(conv1_ref, conv2_ref, tall1, tall2, taps1, taps2)
+    for f in range(2):
+        odd[f, 0] = jnp.zeros((64, 10 * CIN), jnp.bfloat16)
+        near[f, 0] = jnp.zeros((64, 9 * C1), jnp.bfloat16)
+        near[f, 9] = jnp.zeros((64, 9 * C1), jnp.bfloat16)
     for chunk in range(CHUNKS):
         gathered[chunk, 0] = jnp.zeros((part, C2), jnp.bfloat16)
         gathered[chunk, FRAMES + 1] = jnp.zeros((part, C2), jnp.bfloat16)
-        gathered[chunk, pl.ds(1 + f_dev * me, f_dev)] = second_ref[:, cells_of(me, chunk), :]
+    for pair in range(pairs):
+        convolve_pair(
+            pair,
+            f_dev * me,
+            length,
+            occupancy_ref,
+            picks1,
+            picks2,
+            taps1,
+            taps2,
+            even,
+            odd,
+            maps,
+            near,
+            second,
+        )
+        if pair == 0:
+            pl.semaphore_wait(barrier, count - 1 + scenes - 1)
+        for chunk in range(CHUNKS):
+            each(1, count, lambda d, chunk=chunk, pair=pair: there(chunk, pair, d).start())
+    for chunk in range(CHUNKS):
+        gathered[chunk, pl.ds(1 + f_dev * me, f_dev)] = second[:, cells_of(me, chunk), :]
 
     span = 256 // part
     block = span * part
@@ -183,7 +292,8 @@
     total[...] = jnp.zeros_like(total)
 
     for chunk in range(CHUNKS):
-        each(1, count, lambda d, chunk=chunk: there(chunk, d).wait_recv())
+        for pair in range(pairs):
+            each(1, count, lambda d, chunk=chunk, pair=pair: there(chunk, pair, d).wait_recv())
 
         def project(b, carry, chunk=chunk):
             window = gathered[chunk, pl.ds(b * span, span + 2)].reshape((span + 2) * part, C2)
@@ -279,7 +389,8 @@
     loss_ref[...] = jnp.sum(scene_sums[...], axis=0)
     each(1, scenes, lambda d: scene_sum(d).wait_send())
     for chunk in range(CHUNKS):
-        each(1, count, lambda d, chunk=chunk: there(chunk, d).wait_send())
+        for pair in range(pairs):
+            each(1, count, lambda d, chunk=chunk, pair=pair: there(chunk, pair, d).wait_send())
         each(1, count, lambda d, chunk=chunk: back(chunk, d).wait_send())
 
 
@@ -295,19 +406,7 @@
     out_weight,
 ):
     f_dev = occupancy.shape[1]
-    length = scene_lengths[0]
     count, scenes = lax.axis_size("frame"), lax.axis_size("scene")
-    first_frame = lax.axis_index("frame") * f_dev
-    frame_ids = first_frame + jnp.arange(f_dev, dtype=jnp.int32)
-    valid_rows = (frame_ids < length).astype(jnp.float32)
-    voxels = occupancy[0].reshape(f_dev, CIN, HI, HI, ZD)
-    first_maps = jax.nn.silu(spatial_conv(voxels, conv1_weight, CIN, 2)).astype(jnp.bfloat16)
-    second_full = jax.nn.silu(spatial_conv(first_maps, conv2_weight, C1, 1))
-    second_maps = (second_full.reshape(f_dev, C2, CELLS) * valid_rows[:, None, None]).astype(
-        jnp.bfloat16
-    )
-    second = second_maps.transpose(0, 2, 1)
-
     part = CELLS // count // CHUNKS
     rows = FRAMES * part
     wide_rows = pltpu.VMEM((2, rows, 128), jnp.float32)
@@ -318,9 +417,18 @@
             jax.ShapeDtypeStruct((f_dev, C2, CELLS), jnp.bfloat16),
             jax.ShapeDtypeStruct((8, 128), jnp.float32),
         ),
-        in_specs=[pl.BlockSpec(memory_space=pltpu.SMEM)] + [in_vmem] * 6,
+        in_specs=[pl.BlockSpec(memory_space=pltpu.SMEM)] + [in_vmem] * 10,
         out_specs=(in_vmem, in_vmem),
         scratch_shapes=[
+            pltpu.VMEM((CIN * 27, C1), jnp.float32),
+            pltpu.VMEM((2, C1 * 27, 128), jnp.float32),
+            pltpu.VMEM((3, 10 * CIN, C1), jnp.bfloat16),
+            pltpu.VMEM((3, 9 * C1, C2), jnp.bfloat16),
+            pltpu.VMEM((2, 8, 64, 10 * CIN), jnp.bfloat16),
+            pltpu.VMEM((2, 9, 64, 10 * CIN), jnp.bfloat16),
+            pltpu.VMEM((CELLS, 2 * C1), jnp.bfloat16),
+            pltpu.VMEM((2, 10, 64, 9 * C1), jnp.bfloat16),
+            pltpu.VMEM((f_dev, CELLS, C2), jnp.bfloat16),
             pltpu.VMEM((CHUNKS, FRAMES + 2, part, C2), jnp.bfloat16),
             pltpu.VMEM((rows, C2), jnp.bfloat16),
             wide_rows,
@@ -333,13 +441,26 @@
             pltpu.VMEM((count, 8, 128), jnp.float32),
             pltpu.VMEM((scenes, 8, 128), jnp.float32),
         ]
-        + [pltpu.SemaphoreType.DMA((CHUNKS, count))] * 4
+        + [pltpu.SemaphoreType.DMA((CHUNKS * f_dev // 2, count))] * 2
+        + [pltpu.SemaphoreType.DMA((CHUNKS, count))] * 2
         + [pltpu.SemaphoreType.DMA((count,))] * 2
         + [pltpu.SemaphoreType.DMA((scenes,))] * 2,
         compiler_params=pltpu.CompilerParams(
             collective_id=0, has_side_effects=True, vmem_limit_bytes=48 * 2**20
         ),
-    )(scene_lengths, second, temporal_weight, query_weight, key_weight, value_weight, out_weight)
+    )(
+        scene_lengths,
+        occupancy[0],
+        conv1_weight.T,
+        conv2_weight,
+        jnp.asarray(picks_strided(), jnp.bfloat16),
+        jnp.asarray(picks_near(), jnp.bfloat16),
+        temporal_weight,
+        query_weight,
+        key_weight,
+        value_weight,
+        out_weight,
+    )
     slot_count = float(scenes * FRAMES * CELLS * C2)
     kl_loss = 0.5 * jnp.sum(sums) / slot_count
     return (encoded[None], kl_loss)

time: 89.6 us -> 77.5 us (0.86)
  matrix products: 15.8 us -> 0 us
  Pallas kernels: 56.7 us -> 62.3 us
  other arithmetic: 2.98 us -> 0.6 us
    conv_general_dilated x1 -> x0, matrix products: 15.8 us -> none  [spatial_conv(): lax.conv_general_dilated(voxels, kernel, (stride, stride, 1), ((1, 1), (1...]
    pallas_call x1, Pallas kernels: 56.7 us -> 62.3 us  [shards(): pl.pallas_call(functools.partial(mixing_kernel, count, scenes), out_shape...]
    unnamed x17 -> x21, local copies, waits for them, and re-layouts: 6.25 us -> 11.1 us
    reshape x2 -> x0, local copies, waits for them, and re-layouts: 4.35 us -> none  [spatial_conv(): kernel = weight.reshape(channels_out, channels_in, 3, 3, 3)]
    mul x1 -> x0, other arithmetic: 2.14 us -> none  [shards(): second_full = jax.nn.silu(spatial_conv(first_maps, conv2_weight, C1, 1))]
where the time goes in v3:
time: 77.5 us; the launch traced here: 77.1 us
  Pallas kernels  62.3 us (80%)
  local copies, waits for them, and re-layouts  11.1 us (14%)
  between operations  3.09 us (4%)
    pallas_call x1, Pallas kernels, shards(): pl.pallas_call(functools.partial(mixing_kernel, count, scenes), out_shape...  62.3 us
    unnamed x21, local copies, waits for them, and re-layouts  11.1 us

profile of v3, /device:TPU:1, one launch (start us, length us, event | category | flops | bytes accessed | tf_op | source)
XLA Modules:
  0.0 77.1 jit_solution(11881604873476735837)
XLA Ops:
  1.3 0.0 copy-start
  1.3 1.5 %copy-done = bf16[256,3456]{1,0:T(8,128)(2,1)S(1)} copy-done((bf16[256,3456]{1,0:T(8,128)(2,1)S(1)}, bf16[256,3456]{1,0:T(8,128)(2,1)}, u32[]{:S(2)}) %copy-start) | copy-done | bytes 1769496
  2.8 0.0 copy-start.1
  2.8 1.2 %copy-done.1 = bf16[1,4,64,2048]{3,2,1,0:T(8,128)(2,1)S(1)} copy-done((bf16[1,4,64,2048]{3,2,1,0:T(8,128)(2,1)S(1)}, bf16[1,4,64,2048]{3,2,1,0:T(8,128)(2,1)}, u32[]{:S(2)}) %copy-start.1) | copy-done | bytes 1048600
  4.0 0.0 copy-start.2
  4.0 1.0 %copy-done.2 = bf16[128,1728]{0,1:T(8,128)(2,1)S(1)} copy-done((bf16[128,1728]{0,1:T(8,128)(2,1)S(1)}, bf16[128,1728]{0,1:T(8,128)(2,1)}, u32[]{:S(2)}) %copy-start.2) | copy-done | bytes 442392
  5.0 0.0 copy-start.3
  5.0 1.0 %copy-done.3 = bf16[3,256,256]{2,1,0:T(8,128)(2,1)S(1)} copy-done((bf16[3,256,256]{2,1,0:T(8,128)(2,1)S(1)}, bf16[3,256,256]{2,1,0:T(8,128)(2,1)}, u32[]{:S(2)}) %copy-start.3) | copy-done | bytes 393240
  6.0 0.0 copy-start.4
  6.0 0.9 %copy-done.4 = bf16[320,256]{1,0:T(8,128)(2,1)S(1)} copy-done((bf16[320,256]{1,0:T(8,128)(2,1)S(1)}, bf16[320,256]{1,0:T(8,128)(2,1)}, u32[]{:S(2)}) %copy-start.4) | copy-done | bytes 163864
  6.9 0.0 copy-start.5
  6.9 0.9 %copy-done.5 = bf16[576,64]{1,0:T(8,128)(2,1)S(1)} copy-done((bf16[576,64]{1,0:T(8,128)(2,1)S(1)}, bf16[576,64]{1,0:T(8,128)(2,1)}, u32[]{:S(2)}) %copy-start.5) | copy-done | bytes 73752
  7.8 0.0 copy-start.6
  7.8 0.9 %copy-done.6 = bf16[256,256]{1,0:T(8,128)(2,1)S(1)} copy-done((bf16[256,256]{1,0:T(8,128)(2,1)S(1)}, bf16[256,256]{1,0:T(8,128)(2,1)}, u32[]{:S(2)}) %copy-start.6) | copy-done | bytes 131096
  8.7 0.0 copy-start.7
  8.7 0.9 %copy-done.7 = bf16[256,256]{1,0:T(8,128)(2,1)S(1)} copy-done((bf16[256,256]{1,0:T(8,128)(2,1)S(1)}, bf16[256,256]{1,0:T(8,128)(2,1)}, u32[]{:S(2)}) %copy-start.7) | copy-done | bytes 131096
  9.6 0.0 copy-start.8
  9.6 0.9 %copy-done.8 = bf16[256,256]{1,0:T(8,128)(2,1)S(1)} copy-done((bf16[256,256]{1,0:T(8,128)(2,1)S(1)}, bf16[256,256]{1,0:T(8,128)(2,1)}, u32[]{:S(2)}) %copy-start.8) | copy-done | bytes 131096
  10.5 0.0 copy-start.9
  10.5 0.9 %copy-done.9 = bf16[256,256]{1,0:T(8,128)(2,1)S(1)} copy-done((bf16[256,256]{1,0:T(8,128)(2,1)S(1)}, bf16[256,256]{1,0:T(8,128)(2,1)}, u32[]{:S(2)}) %copy-start.9) | copy-done | bytes 131096
  11.4 62.3 %shard_map.122 = (bf16[4,256,512]{2,1,0:T(8,128)(2,1)S(1)}, f32[8,128]{1,0:T(8,128)S(1)}) custom-call(s32[1]{0:T(128)S(6)} %copy.14.length_ref, bf16[4,64,2048]{2,1,0:T(8,128)(2,1)S(1)} %bitcast.3, bf16[1728,128]{1,0:T(8,128)(2,1)S(1)} %bitcast.5, bf16[256,3456]{1,0:T(8,128)(2,1)S(1)} %copy-done, bf16[320,256]{1,0:T(8,128)(2,1)S(1)} %copy-done.4, ...), custom_call_target="tpu_custom_call" | custom-call | tf_op jit(solution)/shard_map/pallas_call | solution.py:414
  73.7 0.6 reduce_sum.9
  75.0 1.0 %copy.15 = bf16[1,4,256,512]{3,2,1,0:T(8,128)(2,1)} copy(bf16[1,4,256,512]{3,2,1,0:T(8,128)(2,1)S(1)} %bitcast.4) | data formatting | bytes 2097152
Async XLA Ops:
  1.3 1.5 %copy-start = (bf16[256,3456]{1,0:T(8,128)(2,1)S(1)}, bf16[256,3456]{1,0:T(8,128)(2,1)}, u32[]{:S(2)}) copy-start(bf16[256,3456]{1,0:T(8,128)(2,1)} %conv2_ref.1) | copy-start | bytes 5308420
  2.8 1.2 %copy-start.1 = (bf16[1,4,64,2048]{3,2,1,0:T(8,128)(2,1)S(1)}, bf16[1,4,64,2048]{3,2,1,0:T(8,128)(2,1)}, u32[]{:S(2)}) copy-start(bf16[1,4,64,2048]{3,2,1,0:T(8,128)(2,1)} %param.11) | copy-start | bytes 3145732
  4.0 1.0 %copy-start.2 = (bf16[128,1728]{0,1:T(8,128)(2,1)S(1)}, bf16[128,1728]{0,1:T(8,128)(2,1)}, u32[]{:S(2)}) copy-start(bf16[128,1728]{0,1:T(8,128)(2,1)} %param.13) | copy-start | bytes 1327108
  5.0 1.0 %copy-start.3 = (bf16[3,256,256]{2,1,0:T(8,128)(2,1)S(1)}, bf16[3,256,256]{2,1,0:T(8,128)(2,1)}, u32[]{:S(2)}) copy-start(bf16[3,256,256]{2,1,0:T(8,128)(2,1)} %temporal_ref.1) | copy-start | bytes 1179652
  6.0 0.9 %copy-start.4 = (bf16[320,256]{1,0:T(8,128)(2,1)S(1)}, bf16[320,256]{1,0:T(8,128)(2,1)}, u32[]{:S(2)}) copy-start(bf16[320,256]{1,0:T(8,128)(2,1)} %constant.11.clone.picks1) | copy-start | bytes 491524
  6.9 0.9 %copy-start.5 = (bf16[576,64]{1,0:T(8,128)(2,1)S(1)}, bf16[576,64]{1,0:T(8,128)(2,1)}, u32[]{:S(2)}) copy-start(bf16[576,64]{1,0:T(8,128)(2,1)} %constant.12.clone.picks2) | copy-start | bytes 221188
  7.8 0.9 %copy-start.6 = (bf16[256,256]{1,0:T(8,128)(2,1)S(1)}, bf16[256,256]{1,0:T(8,128)(2,1)}, u32[]{:S(2)}) copy-start(bf16[256,256]{1,0:T(8,128)(2,1)} %query_ref.1) | copy-start | bytes 393220
  8.7 0.9 %copy-start.7 = (bf16[256,256]{1,0:T(8,128)(2,1)S(1)}, bf16[256,256]{1,0:T(8,128)(2,1)}, u32[]{:S(2)}) copy-start(bf16[256,256]{1,0:T(8,128)(2,1)} %key_ref.1) | copy-start | bytes 393220
  9.6 0.9 %copy-start.8 = (bf16[256,256]{1,0:T(8,128)(2,1)S(1)}, bf16[256,256]{1,0:T(8,128)(2,1)}, u32[]{:S(2)}) copy-start(bf16[256,256]{1,0:T(8,128)(2,1)} %value_ref.1) | copy-start | bytes 393220
  10.5 0.9 %copy-start.9 = (bf16[256,256]{1,0:T(8,128)(2,1)S(1)}, bf16[256,256]{1,0:T(8,128)(2,1)}, u32[]{:S(2)}) copy-start(bf16[256,256]{1,0:T(8,128)(2,1)} %out_weight_ref.1) | copy-start | bytes 393220

commit v4 on v3

--- a/solution.py
+++ b/solution.py
@@ -124,18 +124,28 @@
     count,
     scenes,
     length_ref,
+    occupancy_in,
+    picks1_in,
+    conv1_in,
+    conv2_in,
+    picks2_in,
+    temporal_in,
+    query_in,
+    key_in,
+    value_in,
+    out_weight_in,
+    encoded_ref,
+    loss_ref,
     occupancy_ref,
+    picks1,
     conv1_ref,
     conv2_ref,
-    picks1,
     picks2,
     temporal_ref,
     query_ref,
     key_ref,
     value_ref,
     out_weight_ref,
-    encoded_ref,
-    loss_ref,
     tall1,
     tall2,
     taps1,
@@ -164,6 +174,7 @@
     frame_recv,
     scene_send,
     scene_recv,
+    load_sem,
 ):
     f_dev = occupancy_ref.shape[0]
     pairs = f_dev // 2
@@ -174,6 +185,26 @@
     my_scene = lax.axis_index("scene")
     length = length_ref[0]
 
+    loads = [
+        pltpu.make_async_copy(source, into, load_sem.at[i])
+        for i, (source, into) in enumerate(
+            (
+                (occupancy_in, occupancy_ref),
+                (picks1_in, picks1),
+                (conv1_in, conv1_ref),
+                (conv2_in, conv2_ref),
+                (picks2_in, picks2),
+                (temporal_in, temporal_ref),
+                (query_in, query_ref),
+                (key_in, key_ref),
+                (value_in, value_ref),
+                (out_weight_in, out_weight_ref),
+            )
+        )
+    ]
+    for load in loads:
+        load.start()
+
     barrier = pltpu.get_barrier_semaphore()
 
     def greet_frame(d, carry):
@@ -249,6 +280,8 @@
 
         lax.fori_loop(first, last, step, 0)
 
+    for load in loads[:5]:
+        load.wait()
     order_weights(conv1_ref, conv2_ref, tall1, tall2, taps1, taps2)
     for f in range(2):
         odd[f, 0] = jnp.zeros((64, 10 * CIN), jnp.bfloat16)
@@ -280,6 +313,9 @@
     for chunk in range(CHUNKS):
         gathered[chunk, pl.ds(1 + f_dev * me, f_dev)] = second[:, cells_of(me, chunk), :]
 
+    for load in loads[5:]:
+        load.wait()
+
     span = 256 // part
     block = span * part
     head_of = lax.broadcasted_iota(jnp.int32, (FRAMES, C2), 1) // HD
@@ -313,7 +349,7 @@
                 into[1, at, :] = made[:, 128:]
             return carry
 
-        lax.fori_loop(0, FRAMES // span, project, 0)
+        lax.fori_loop(0, FRAMES // span, project, 0, unroll=True)
 
         def cell_rows(ref, cell):
             at = pl.ds(cell, FRAMES, stride=part)
@@ -344,7 +380,7 @@
             att_rows[1, at, :] = attended[:, 128:]
             return carry
 
-        lax.fori_loop(0, part, attend, 0)
+        lax.fori_loop(0, part, attend, 0, unroll=True)
 
         def finish(b, carry, chunk=chunk):
             at = pl.ds(pl.multiple_of(b * block, block), block)
@@ -360,7 +396,7 @@
             total[...] += squares[:, :128] + squares[:, 128:]
             return carry
 
-        lax.fori_loop(0, FRAMES // span, finish, 0)
+        lax.fori_loop(0, FRAMES // span, finish, 0, unroll=True)
         each(1, count, lambda d, chunk=chunk: back(chunk, d).start())
         returned[:, cells_of(me, chunk), :] = done_rows[chunk, pl.ds(f_dev * me, f_dev)]
 
@@ -372,18 +408,11 @@
     each(1, scenes, lambda d: scene_sum(d).start())
     scene_sums[my_scene] = total[...]
 
-    eye = (
-        lax.broadcasted_iota(jnp.int32, (C2, C2), 0)
-        == lax.broadcasted_iota(jnp.int32, (C2, C2), 1)
-    ).astype(jnp.bfloat16)
     for chunk in range(CHUNKS):
         each(1, count, lambda d, chunk=chunk: back(chunk, d).wait_recv())
 
-    def turn(f, carry):
-        encoded_ref[f] = by_rows(eye, returned[f]).astype(jnp.bfloat16)
-        return carry
-
-    lax.fori_loop(0, f_dev, turn, 0)
+    for f in range(f_dev):
+        encoded_ref[f] = returned[f].T
 
     each(1, scenes, lambda d: scene_sum(d).wait_recv())
     loss_ref[...] = jnp.sum(scene_sums[...], axis=0)
@@ -407,6 +436,18 @@
 ):
     f_dev = occupancy.shape[1]
     count, scenes = lax.axis_size("frame"), lax.axis_size("scene")
+    operands = (
+        occupancy[0],
+        jnp.asarray(picks_strided(), jnp.bfloat16),
+        conv1_weight.T,
+        conv2_weight,
+        jnp.asarray(picks_near(), jnp.bfloat16),
+        temporal_weight,
+        query_weight,
+        key_weight,
+        value_weight,
+        out_weight,
+    )
     part = CELLS // count // CHUNKS
     rows = FRAMES * part
     wide_rows = pltpu.VMEM((2, rows, 128), jnp.float32)
@@ -417,9 +458,10 @@
             jax.ShapeDtypeStruct((f_dev, C2, CELLS), jnp.bfloat16),
             jax.ShapeDtypeStruct((8, 128), jnp.float32),
         ),
-        in_specs=[pl.BlockSpec(memory_space=pltpu.SMEM)] + [in_vmem] * 10,
+        in_specs=[pl.BlockSpec(memory_space=pltpu.SMEM)] + [pl.BlockSpec(memory_space=pl.ANY)] * 10,
         out_specs=(in_vmem, in_vmem),
-        scratch_shapes=[
+        scratch_shapes=[pltpu.VMEM(array.shape, array.dtype) for array in operands]
+        + [
             pltpu.VMEM((CIN * 27, C1), jnp.float32),
             pltpu.VMEM((2, C1 * 27, 128), jnp.float32),
             pltpu.VMEM((3, 10 * CIN, C1), jnp.bfloat16),
@@ -444,23 +486,12 @@
         + [pltpu.SemaphoreType.DMA((CHUNKS * f_dev // 2, count))] * 2
         + [pltpu.SemaphoreType.DMA((CHUNKS, count))] * 2
         + [pltpu.SemaphoreType.DMA((count,))] * 2
-        + [pltpu.SemaphoreType.DMA((scenes,))] * 2,
+        + [pltpu.SemaphoreType.DMA((scenes,))] * 2
+        + [pltpu.SemaphoreType.DMA((10,))],
         compiler_params=pltpu.CompilerParams(
-            collective_id=0, has_side_effects=True, vmem_limit_bytes=48 * 2**20
+            collective_id=0, has_side_effects=True, vmem_limit_bytes=60 * 2**20
         ),
-    )(
-        scene_lengths,
-        occupancy[0],
-        conv1_weight.T,
-        conv2_weight,
-        jnp.asarray(picks_strided(), jnp.bfloat16),
-        jnp.asarray(picks_near(), jnp.bfloat16),
-        temporal_weight,
-        query_weight,
-        key_weight,
-        value_weight,
-        out_weight,
-    )
+    )(scene_lengths, *operands)
     slot_count = float(scenes * FRAMES * CELLS * C2)
     kl_loss = 0.5 * jnp.sum(sums) / slot_count
     return (encoded[None], kl_loss)

time: 77.5 us -> 58 us (0.75)
  Pallas kernels: 62.3 us -> 51.2 us
  local copies, waits for them, and re-layouts: 11.1 us -> 2.26 us
    pallas_call x1, Pallas kernels: 62.3 us -> 51.2 us  [shards(): pl.pallas_call(functools.partial(mixing_kernel, count, scenes), out_shape...]
    unnamed x21 -> x1, local copies, waits for them, and re-layouts: 11.1 us -> 2.26 us
where the time goes in v4:
time: 58 us; the launch traced here: 57.8 us
  Pallas kernels  51.2 us (88%)
  between operations  3.07 us (5%)
  local copies, waits for them, and re-layouts  2.26 us (4%)
  other arithmetic  1.28 us (2%)
    pallas_call x1, Pallas kernels, shards(): pl.pallas_call(functools.partial(mixing_kernel, count, scenes), out_shape...  51.2 us
    unnamed x1, local copies, waits for them, and re-layouts  2.26 us
    reduce_sum x1, other arithmetic, shards(): kl_loss = 0.5 * jnp.sum(sums) / slot_count  1.28 us

profile of v4, /device:TPU:1, one launch (start us, length us, event | category | flops | bytes accessed | tf_op | source)
XLA Modules:
  0.0 57.8 jit_solution(3558436891213203378)
XLA Ops:
  1.3 51.2 %shard_map.122 = (bf16[4,256,512]{2,1,0:T(8,128)(2,1)}, f32[8,128]{1,0:T(8,128)}) custom-call(s32[1]{0:T(128)S(6)} %copy.14.length_ref, bf16[4,64,2048]{2,1,0:T(8,128)(2,1)} %bitcast.3, bf16[320,256]{1,0:T(8,128)(2,1)} %constant.11.clone.picks1_in, bf16[1728,128]{1,0:T(8,128)(2,1)} %bitcast.5, bf16[256,3456]{1,0:T(8,128)(2,1)} %conv2_in.1, ...), custom_call_target="tpu_custom_call" | custom-call | tf_op jit(solution)/shard_map/pallas_call | solution.py:455
  52.5 1.3 %reduce_sum.9 = f32[]{:T(128)} reduce(f32[8,128]{1,0:T(8,128)} %get-tuple-element.5, f32[]{:T(128)} %constant.4.clone.1), dimensions={0,1}, to_apply=%region_0.0 | reduce | flops 1023 | bytes 4104 | tf_op jit(solution)/shard_map/reduce_sum | solution.py:496
  54.4 2.3 %copy.15 = bf16[1,4,256,512]{3,2,1,0:T(8,128)(2,1)} copy(bf16[1,4,256,512]{3,2,1,0:T(8,128)(2,1)} %bitcast.4) | data formatting | bytes 2097152

commit v5 on v4

--- a/solution.py
+++ b/solution.py
@@ -23,6 +23,25 @@
 
 FRAMES = 64
 CHUNKS = 2
+SIDE = 4
+HALF_WAY = 8
+OFFSETS = (
+    (2, 2),
+    (2, 1),
+    (2, 3),
+    (1, 2),
+    (3, 2),
+    (2, 0),
+    (0, 2),
+    (1, 1),
+    (3, 3),
+    (1, 3),
+    (3, 1),
+    (0, 1),
+    (0, 3),
+    (1, 0),
+    (3, 0),
+)
 LOG2_E = 1.4426950408889634
 
 
@@ -62,29 +81,34 @@
     return picks.reshape(9 * 64, 64)
 
 
-def order_weights(conv1_ref, conv2_ref, tall1, tall2, taps1, taps2):
+def order_first(conv1_ref, tall1, taps1):
+    tall1[...] = conv1_ref[...].astype(jnp.float32)
+    for dx in range(3):
+        for tap in range(9):
+            at = pl.ds(dx * 9 + tap, CIN, stride=27)
+            taps1[dx, tap * CIN : (tap + 1) * CIN, :] = tall1[at, :].astype(jnp.bfloat16)
+        taps1[dx, 9 * CIN :, :] = jnp.zeros((CIN, C1), jnp.bfloat16)
+
+
+def order_second(conv2_ref, tall2, taps2):
     eye = (
         lax.broadcasted_iota(jnp.int32, (128, 128), 0)
         == lax.broadcasted_iota(jnp.int32, (128, 128), 1)
     ).astype(jnp.bfloat16)
-    tall1[...] = conv1_ref[...].astype(jnp.float32)
     for at in range(0, C1 * 27, 128):
         turned = by_rows(eye, conv2_ref[:, at : at + 128])
         tall2[0, at : at + 128, :] = turned[:, :128]
         tall2[1, at : at + 128, :] = turned[:, 128:]
     for dx in range(3):
         for tap in range(9):
-            at = pl.ds(dx * 9 + tap, CIN, stride=27)
-            taps1[dx, tap * CIN : (tap + 1) * CIN, :] = tall1[at, :].astype(jnp.bfloat16)
             at = pl.ds(dx * 9 + tap, C1, stride=27)
             taps2[dx, tap * C1 : (tap + 1) * C1, :] = jnp.concatenate(
                 [tall2[0, at, :], tall2[1, at, :]], axis=1
             ).astype(jnp.bfloat16)
-        taps1[dx, 9 * CIN :, :] = jnp.zeros((CIN, C1), jnp.bfloat16)
 
 
 def convolve_pair(
-    pair, first_frame, length, occupancy_ref, picks1, picks2, taps1, taps2, even, odd, maps, near, second
+    pair, first_frame, length, ready, send, occupancy_ref, picks1, picks2, taps1, taps2, even, odd, maps, near, second
 ):
     blank = jnp.zeros((CIN, 128), jnp.bfloat16)
     for x in range(HI):
@@ -100,11 +124,13 @@
                 into[f, row, :, k * 128 : (k + 1) * 128] = found[
                     k * 64 : (k + 1) * 64, f * 128 : (f + 1) * 128
                 ]
+    ready(1)
     for f in range(2):
-        total = by_columns(odd[f, 0:8].reshape(CELLS, 10 * CIN), taps1[0])
-        total = total + by_columns(even[f].reshape(CELLS, 10 * CIN), taps1[1])
-        total = total + by_columns(odd[f, 1:9].reshape(CELLS, 10 * CIN), taps1[2])
+        planes = [odd[f, 0:8], even[f], odd[f, 1:9]]
+        planes = jnp.concatenate([p.reshape(CELLS, 10 * CIN) for p in planes], axis=1)
+        total = by_columns(planes, taps1[...].reshape(30 * CIN, C1))
         maps[:, f * C1 : (f + 1) * C1] = silu(total).astype(jnp.bfloat16)
+    ready(2)
     for x in range(8):
         found = by_columns(picks2[...], maps[x * 64 : (x + 1) * 64, :]).astype(jnp.bfloat16)
         for f in range(2):
@@ -113,11 +139,11 @@
                     k * 64 : (k + 1) * 64, f * C1 : (f + 1) * C1
                 ]
     for f in range(2):
-        total = by_columns(near[f, 0:8].reshape(CELLS, 9 * C1), taps2[0])
-        total = total + by_columns(near[f, 1:9].reshape(CELLS, 9 * C1), taps2[1])
-        total = total + by_columns(near[f, 2:10].reshape(CELLS, 9 * C1), taps2[2])
+        planes = [near[f, dx : dx + 8].reshape(CELLS, 9 * C1) for dx in range(3)]
+        total = by_columns(jnp.concatenate(planes, axis=1), taps2[...].reshape(27 * C1, C2))
         kept = jnp.where(first_frame + 2 * pair + f < length, silu(total), 0.0)
         second[2 * pair + f] = kept.astype(jnp.bfloat16)
+        send(2 * pair + f)
 
 
 def mixing_kernel(
@@ -164,6 +190,7 @@
     done_rows,
     returned,
     total,
+    group_total,
     frame_sums,
     scene_sums,
     there_send,
@@ -231,19 +258,29 @@
     def cells_of(device, chunk):
         return pl.ds(pl.multiple_of(device * cells + chunk * part, part), part)
 
-    def there(chunk, pair, d):
-        to = lax.rem(me + d, count)
+    pieces = [(frame, 1, 0, cells) for frame in range(f_dev - 2)]
+    pieces += [(f_dev - 2, 2, chunk * part, part) for chunk in range(CHUNKS)]
+
+    def peer(d):
+        down, across = OFFSETS[d - 1]
+        return lax.rem(me // SIDE + down, SIDE) * SIDE + lax.rem(me + across, SIDE)
+
+    def there(piece, d):
+        frame, frames, first, size = pieces[piece]
+        to = peer(d)
         return pltpu.make_async_remote_copy(
-            src_ref=second.at[pl.ds(2 * pair, 2), cells_of(to, chunk), :],
-            dst_ref=gathered.at[chunk, pl.ds(1 + f_dev * me + 2 * pair, 2)],
-            send_sem=there_send.at[chunk * pairs + pair, d],
-            recv_sem=there_recv.at[chunk * pairs + pair, d],
+            src_ref=second.at[
+                pl.ds(frame, frames), pl.ds(pl.multiple_of(to * cells + first, part), size), :
+            ],
+            dst_ref=gathered.at[pl.ds(1 + f_dev * me + frame, frames), pl.ds(first, size)],
+            send_sem=there_send.at[piece, d],
+            recv_sem=there_recv.at[piece, d],
             device_id={"frame": to},
             device_id_type=pl.DeviceIdType.MESH,
         )
 
     def back(chunk, d):
-        to = lax.rem(me + d, count)
+        to = peer(d)
         return pltpu.make_async_remote_copy(
             src_ref=done_rows.at[chunk, pl.ds(f_dev * to, f_dev)],
             dst_ref=returned.at[:, cells_of(me, chunk), :],
@@ -259,13 +296,13 @@
             dst_ref=frame_sums.at[me],
             send_sem=frame_send.at[d],
             recv_sem=frame_recv.at[d],
-            device_id={"frame": lax.rem(me + d, count)},
+            device_id={"frame": peer(d)},
             device_id_type=pl.DeviceIdType.MESH,
         )
 
     def scene_sum(d):
         return pltpu.make_async_remote_copy(
-            src_ref=total,
+            src_ref=group_total,
             dst_ref=scene_sums.at[my_scene],
             send_sem=scene_send.at[d],
             recv_sem=scene_recv.at[d],
@@ -274,27 +311,41 @@
         )
 
     def each(first, last, act):
-        def step(d, carry):
+        for d in range(first, last):
             act(d)
-            return carry
-
-        lax.fori_loop(first, last, step, 0)
-
-    for load in loads[:5]:
+
+    for load in loads[:2]:
         load.wait()
-    order_weights(conv1_ref, conv2_ref, tall1, tall2, taps1, taps2)
+
+    def ready(stage):
+        if stage == 1:
+            loads[2].wait()
+            order_first(conv1_ref, tall1, taps1)
+        else:
+            loads[3].wait()
+            loads[4].wait()
+            order_second(conv2_ref, tall2, taps2)
+
+    def send(frame):
+        if frame == 0:
+            pl.semaphore_wait(barrier, count - 1 + scenes - 1)
+        for piece in range(len(pieces)):
+            if pieces[piece][0] + pieces[piece][1] == frame + 1:
+                each(1, count, lambda d, piece=piece: there(piece, d).start())
+
     for f in range(2):
         odd[f, 0] = jnp.zeros((64, 10 * CIN), jnp.bfloat16)
         near[f, 0] = jnp.zeros((64, 9 * C1), jnp.bfloat16)
         near[f, 9] = jnp.zeros((64, 9 * C1), jnp.bfloat16)
-    for chunk in range(CHUNKS):
-        gathered[chunk, 0] = jnp.zeros((part, C2), jnp.bfloat16)
-        gathered[chunk, FRAMES + 1] = jnp.zeros((part, C2), jnp.bfloat16)
+    gathered[0] = jnp.zeros((cells, C2), jnp.bfloat16)
+    gathered[FRAMES + 1] = jnp.zeros((cells, C2), jnp.bfloat16)
     for pair in range(pairs):
         convolve_pair(
             pair,
             f_dev * me,
             length,
+            ready if pair == 0 else lambda stage: None,
+            send,
             occupancy_ref,
             picks1,
             picks2,
@@ -306,12 +357,9 @@
             near,
             second,
         )
-        if pair == 0:
-            pl.semaphore_wait(barrier, count - 1 + scenes - 1)
-        for chunk in range(CHUNKS):
-            each(1, count, lambda d, chunk=chunk, pair=pair: there(chunk, pair, d).start())
-    for chunk in range(CHUNKS):
-        gathered[chunk, pl.ds(1 + f_dev * me, f_dev)] = second[:, cells_of(me, chunk), :]
+    gathered[pl.ds(1 + f_dev * me, f_dev)] = second[
+        :, pl.ds(pl.multiple_of(me * cells, cells), cells), :
+    ]
 
     for load in loads[5:]:
         load.wait()
@@ -328,11 +376,13 @@
     total[...] = jnp.zeros_like(total)
 
     for chunk in range(CHUNKS):
-        for pair in range(pairs):
-            each(1, count, lambda d, chunk=chunk, pair=pair: there(chunk, pair, d).wait_recv())
+        for piece in range(len(pieces)):
+            if pieces[piece][2] == chunk * part:
+                each(1, count, lambda d, piece=piece: there(piece, d).wait_recv())
 
         def project(b, carry, chunk=chunk):
-            window = gathered[chunk, pl.ds(b * span, span + 2)].reshape((span + 2) * part, C2)
+            window = gathered[pl.ds(b * span, span + 2), chunk * part : (chunk + 1) * part]
+            window = window.reshape((span + 2) * part, C2)
             temporal = by_rows(window[:block], temporal_ref[0])
             temporal = temporal + by_rows(window[part : part + block], temporal_ref[1])
             temporal = temporal + by_rows(window[2 * part :], temporal_ref[2])
@@ -397,16 +447,18 @@
             return carry
 
         lax.fori_loop(0, FRAMES // span, finish, 0, unroll=True)
-        each(1, count, lambda d, chunk=chunk: back(chunk, d).start())
+        if chunk == CHUNKS - 1:
+            each(1, count, lambda d: frame_sum(d).start())
+            frame_sums[me] = total[...]
+            each(1, HALF_WAY, lambda d, chunk=chunk: back(chunk, d).start())
+            each(1, count, lambda d: frame_sum(d).wait_recv())
+            group_total[...] = jnp.sum(frame_sums[...], axis=0)
+            each(1, scenes, lambda d: scene_sum(d).start())
+            scene_sums[my_scene] = group_total[...]
+            each(HALF_WAY, count, lambda d, chunk=chunk: back(chunk, d).start())
+        else:
+            each(1, count, lambda d, chunk=chunk: back(chunk, d).start())
         returned[:, cells_of(me, chunk), :] = done_rows[chunk, pl.ds(f_dev * me, f_dev)]
-
-    each(1, count, lambda d: frame_sum(d).start())
-    frame_sums[me] = total[...]
-    each(1, count, lambda d: frame_sum(d).wait_recv())
-    each(1, count, lambda d: frame_sum(d).wait_send())
-    total[...] = jnp.sum(frame_sums[...], axis=0)
-    each(1, scenes, lambda d: scene_sum(d).start())
-    scene_sums[my_scene] = total[...]
 
     for chunk in range(CHUNKS):
         each(1, count, lambda d, chunk=chunk: back(chunk, d).wait_recv())
@@ -415,11 +467,13 @@
         encoded_ref[f] = returned[f].T
 
     each(1, scenes, lambda d: scene_sum(d).wait_recv())
-    loss_ref[...] = jnp.sum(scene_sums[...], axis=0)
+    slots = float(scenes * FRAMES * CELLS * C2)
+    loss_ref[...] = jnp.sum(jnp.sum(scene_sums[...], axis=0), keepdims=True) * (0.5 / slots)
+    each(1, count, lambda d: frame_sum(d).wait_send())
     each(1, scenes, lambda d: scene_sum(d).wait_send())
+    for piece in range(len(pieces)):
+        each(1, count, lambda d, piece=piece: there(piece, d).wait_send())
     for chunk in range(CHUNKS):
-        for pair in range(pairs):
-            each(1, count, lambda d, chunk=chunk, pair=pair: there(chunk, pair, d).wait_send())
         each(1, count, lambda d, chunk=chunk: back(chunk, d).wait_send())
 
 
@@ -452,11 +506,11 @@
     rows = FRAMES * part
     wide_rows = pltpu.VMEM((2, rows, 128), jnp.float32)
     in_vmem = pl.BlockSpec(memory_space=pltpu.VMEM)
-    encoded, sums = pl.pallas_call(
+    encoded, loss = pl.pallas_call(
         functools.partial(mixing_kernel, count, scenes),
         out_shape=(
             jax.ShapeDtypeStruct((f_dev, C2, CELLS), jnp.bfloat16),
-            jax.ShapeDtypeStruct((8, 128), jnp.float32),
+            jax.ShapeDtypeStruct((1, 1), jnp.float32),
         ),
         in_specs=[pl.BlockSpec(memory_space=pltpu.SMEM)] + [pl.BlockSpec(memory_space=pl.ANY)] * 10,
         out_specs=(in_vmem, in_vmem),
@@ -471,7 +525,7 @@
             pltpu.VMEM((CELLS, 2 * C1), jnp.bfloat16),
             pltpu.VMEM((2, 10, 64, 9 * C1), jnp.bfloat16),
             pltpu.VMEM((f_dev, CELLS, C2), jnp.bfloat16),
-            pltpu.VMEM((CHUNKS, FRAMES + 2, part, C2), jnp.bfloat16),
+            pltpu.VMEM((FRAMES + 2, CELLS // count, C2), jnp.bfloat16),
             pltpu.VMEM((rows, C2), jnp.bfloat16),
             wide_rows,
             wide_rows,
@@ -480,10 +534,11 @@
             pltpu.VMEM((CHUNKS, FRAMES, part, C2), jnp.bfloat16),
             pltpu.VMEM((f_dev, CELLS, C2), jnp.bfloat16),
             pltpu.VMEM((8, 128), jnp.float32),
+            pltpu.VMEM((8, 128), jnp.float32),
             pltpu.VMEM((count, 8, 128), jnp.float32),
             pltpu.VMEM((scenes, 8, 128), jnp.float32),
         ]
-        + [pltpu.SemaphoreType.DMA((CHUNKS * f_dev // 2, count))] * 2
+        + [pltpu.SemaphoreType.DMA((CHUNKS + f_dev - 2, count))] * 2
         + [pltpu.SemaphoreType.DMA((CHUNKS, count))] * 2
         + [pltpu.SemaphoreType.DMA((count,))] * 2
         + [pltpu.SemaphoreType.DMA((scenes,))] * 2
@@ -492,9 +547,7 @@
             collective_id=0, has_side_effects=True, vmem_limit_bytes=60 * 2**20
         ),
     )(scene_lengths, *operands)
-    slot_count = float(scenes * FRAMES * CELLS * C2)
-    kl_loss = 0.5 * jnp.sum(sums) / slot_count
-    return (encoded[None], kl_loss)
+    return (encoded[None], loss.reshape(()))
 
 
 def solution(mesh):

time: 58 us -> 51.9 us (0.89)
  Pallas kernels: 51.2 us -> 46.2 us
  other arithmetic: 1.28 us -> 0 us
    pallas_call x1, Pallas kernels: 51.2 us -> 46.2 us  [shards(): pl.pallas_call(functools.partial(mixing_kernel, count, scenes), out_shape...]
    reduce_sum x1 -> x0, other arithmetic: 1.28 us -> none  [shards(): kl_loss = 0.5 * jnp.sum(sums) / slot_count]
where the time goes in v5:
time: 51.9 us; the launch traced here: 51.5 us
  Pallas kernels  46.2 us (89%)
  between operations  2.98 us (6%)
  local copies, waits for them, and re-layouts  2.26 us (4%)
    pallas_call x1, Pallas kernels, shards(): pl.pallas_call(functools.partial(mixing_kernel, count, scenes), out_shape...  46.2 us
    unnamed x1, local copies, waits for them, and re-layouts  2.26 us

profile of v5, /device:TPU:1, one launch (start us, length us, event | category | flops | bytes accessed | tf_op | source)
XLA Modules:
  0.0 51.5 jit_solution(10841110445652927237)
XLA Ops:
  1.3 46.2 %shard_map.122 = (bf16[4,256,512]{2,1,0:T(8,128)(2,1)}, f32[1,1]{1,0:T(1,128)}) custom-call(s32[1]{0:T(128)S(6)} %copy.15.length_ref, bf16[4,64,2048]{2,1,0:T(8,128)(2,1)} %bitcast.4, bf16[320,256]{1,0:T(8,128)(2,1)} %constant.4.clone.picks1_in, bf16[1728,128]{1,0:T(8,128)(2,1)} %bitcast.6, bf16[256,3456]{1,0:T(8,128)(2,1)} %conv2_in.1, ...), custom_call_target="tpu_custom_call" | custom-call | tf_op jit(solution)/shard_map/pallas_call | solution.py:509
  47.5 2.3 %copy.16 = bf16[1,4,256,512]{3,2,1,0:T(8,128)(2,1)} copy(bf16[1,4,256,512]{3,2,1,0:T(8,128)(2,1)} %bitcast.5) | data formatting | bytes 2097152

commit v6 on v5

--- a/solution.py
+++ b/solution.py
@@ -460,11 +460,15 @@
             each(1, count, lambda d, chunk=chunk: back(chunk, d).start())
         returned[:, cells_of(me, chunk), :] = done_rows[chunk, pl.ds(f_dev * me, f_dev)]
 
-    for chunk in range(CHUNKS):
-        each(1, count, lambda d, chunk=chunk: back(chunk, d).wait_recv())
-
-    for f in range(f_dev):
-        encoded_ref[f] = returned[f].T
+    for down in (2, 1, 3, 0):
+        for d in range(1, count):
+            if OFFSETS[d - 1][0] == down:
+                for chunk in range(CHUNKS):
+                    back(chunk, d).wait_recv()
+        row = lax.rem(me // SIDE + SIDE - down, SIDE)
+        tile = pl.ds(pl.multiple_of(row * SIDE * cells, SIDE * cells), SIDE * cells)
+        for f in range(f_dev):
+            encoded_ref[f, :, tile] = returned[f, tile, :].T
 
     each(1, scenes, lambda d: scene_sum(d).wait_recv())
     slots = float(scenes * FRAMES * CELLS * C2)
@@ -509,8 +513,8 @@
     encoded, loss = pl.pallas_call(
         functools.partial(mixing_kernel, count, scenes),
         out_shape=(
-            jax.ShapeDtypeStruct((f_dev, C2, CELLS), jnp.bfloat16),
-            jax.ShapeDtypeStruct((1, 1), jnp.float32),
+            pltpu.VMEM((f_dev, C2, CELLS), jnp.bfloat16),
+            pltpu.VMEM((1, 1), jnp.float32),
         ),
         in_specs=[pl.BlockSpec(memory_space=pltpu.SMEM)] + [pl.BlockSpec(memory_space=pl.ANY)] * 10,
         out_specs=(in_vmem, in_vmem),

time: 51.9 us -> 49 us (0.944)
  local copies, waits for them, and re-layouts: 2.26 us -> 0.97 us
  Pallas kernels: 46.2 us -> 45.3 us
  between operations: 2.98 us -> 2.45 us
    unnamed x1, local copies, waits for them, and re-layouts: 2.26 us -> 0.97 us
    pallas_call x1, Pallas kernels: 46.2 us -> 45.3 us  [shards(): pl.pallas_call(functools.partial(mixing_kernel, count, scenes), out_shape...]
where the time goes in v6:
time: 49 us; the launch traced here: 48.7 us
  Pallas kernels  45.3 us (92%)
  between operations  2.45 us (5%)
  local copies, waits for them, and re-layouts  0.97 us (2%)
    pallas_call x1, Pallas kernels, shards(): pl.pallas_call(functools.partial(mixing_kernel, count, scenes), out_shape...  45.3 us

profile of v6, /device:TPU:1, one launch (start us, length us, event | category | flops | bytes accessed | tf_op | source)
XLA Modules:
  0.0 48.7 jit_solution(4061790084224224627)
XLA Ops:
  1.3 45.3 %shard_map.122 = (bf16[4,256,512]{2,1,0:T(8,128)(2,1)S(1)}, f32[1,1]{1,0:T(1,128)S(1)}) custom-call(s32[1]{0:T(128)S(6)} %copy.17.length_ref, bf16[4,64,2048]{2,1,0:T(8,128)(2,1)} %bitcast.5, bf16[320,256]{1,0:T(8,128)(2,1)} %constant.4.clone.picks1_in, bf16[1728,128]{1,0:T(8,128)(2,1)} %bitcast.6, bf16[256,3456]{1,0:T(8,128)(2,1)} %conv2_in.1, ...), custom_call_target="tpu_custom_call" | custom-call | tf_op jit(solution)/shard_map/pallas_call | solution.py:513
  46.6 1.0 %copy.15 = bf16[1,4,256,512]{3,2,1,0:T(8,128)(2,1)} copy(bf16[1,4,256,512]{3,2,1,0:T(8,128)(2,1)S(1)} %bitcast.4) | data formatting | bytes 2097152

commit v7 on v6

--- a/solution.py
+++ b/solution.py
@@ -24,7 +24,7 @@
 FRAMES = 64
 CHUNKS = 2
 SIDE = 4
-HALF_WAY = 8
+HALF_WAY = 5
 OFFSETS = (
     (2, 2),
     (2, 1),
@@ -283,7 +283,7 @@
         to = peer(d)
         return pltpu.make_async_remote_copy(
             src_ref=done_rows.at[chunk, pl.ds(f_dev * to, f_dev)],
-            dst_ref=returned.at[:, cells_of(me, chunk), :],
+            dst_ref=returned.at[chunk, me],
             send_sem=back_send.at[chunk, d],
             recv_sem=back_recv.at[chunk, d],
             device_id={"frame": to},
@@ -458,9 +458,17 @@
             each(HALF_WAY, count, lambda d, chunk=chunk: back(chunk, d).start())
         else:
             each(1, count, lambda d, chunk=chunk: back(chunk, d).start())
-        returned[:, cells_of(me, chunk), :] = done_rows[chunk, pl.ds(f_dev * me, f_dev)]
-
+        returned[chunk, me] = done_rows[chunk, pl.ds(f_dev * me, f_dev)]
+
+    for piece in range(len(pieces)):
+        each(1, count, lambda d, piece=piece: there(piece, d).wait_send())
+    each(1, count, lambda d: frame_sum(d).wait_send())
+    each(1, scenes, lambda d: scene_sum(d).wait_send())
+    for chunk in range(CHUNKS - 1):
+        each(1, count, lambda d, chunk=chunk: back(chunk, d).wait_send())
     for down in (2, 1, 3, 0):
+        if down == 0:
+            each(1, count, lambda d: back(CHUNKS - 1, d).wait_send())
         for d in range(1, count):
             if OFFSETS[d - 1][0] == down:
                 for chunk in range(CHUNKS):
@@ -468,17 +476,16 @@
         row = lax.rem(me // SIDE + SIDE - down, SIDE)
         tile = pl.ds(pl.multiple_of(row * SIDE * cells, SIDE * cells), SIDE * cells)
         for f in range(f_dev):
-            encoded_ref[f, :, tile] = returned[f, tile, :].T
+            found = [
+                returned[chunk, row * SIDE + across, f]
+                for across in range(SIDE)
+                for chunk in range(CHUNKS)
+            ]
+            encoded_ref[f, :, tile] = jnp.concatenate(found, axis=0).T
 
     each(1, scenes, lambda d: scene_sum(d).wait_recv())
     slots = float(scenes * FRAMES * CELLS * C2)
     loss_ref[...] = jnp.sum(jnp.sum(scene_sums[...], axis=0), keepdims=True) * (0.5 / slots)
-    each(1, count, lambda d: frame_sum(d).wait_send())
-    each(1, scenes, lambda d: scene_sum(d).wait_send())
-    for piece in range(len(pieces)):
-        each(1, count, lambda d, piece=piece: there(piece, d).wait_send())
-    for chunk in range(CHUNKS):
-        each(1, count, lambda d, chunk=chunk: back(chunk, d).wait_send())
 
 
 def shards(
@@ -536,7 +543,7 @@
             wide_rows,
             wide_rows,
             pltpu.VMEM((CHUNKS, FRAMES, part, C2), jnp.bfloat16),
-            pltpu.VMEM((f_dev, CELLS, C2), jnp.bfloat16),
+            pltpu.VMEM((CHUNKS, count, f_dev, part, C2), jnp.bfloat16),
             pltpu.VMEM((8, 128), jnp.float32),
             pltpu.VMEM((8, 128), jnp.float32),
             pltpu.VMEM((count, 8, 128), jnp.float32),

time: 49 us -> 48.9 us (level)
  no operation moved by 1% of the time
where the time goes in v7:
time: 48.9 us; the launch traced here: 48.6 us
  Pallas kernels  45.1 us (92%)
  between operations  2.45 us (5%)
  local copies, waits for them, and re-layouts  0.97 us (2%)
    pallas_call x1, Pallas kernels, shards(): pl.pallas_call(functools.partial(mixing_kernel, count, scenes), out_shape...  45.1 us

profile of v7, /device:TPU:1, one launch (start us, length us, event | category | flops | bytes accessed | tf_op | source)
XLA Modules:
  0.0 48.6 jit_solution(1559676448690177848)
XLA Ops:
  1.3 45.1 %shard_map.122 = (bf16[4,256,512]{2,1,0:T(8,128)(2,1)S(1)}, f32[1,1]{1,0:T(1,128)S(1)}) custom-call(s32[1]{0:T(128)S(6)} %copy.17.length_ref, bf16[4,64,2048]{2,1,0:T(8,128)(2,1)} %bitcast.5, bf16[320,256]{1,0:T(8,128)(2,1)} %constant.4.clone.picks1_in, bf16[1728,128]{1,0:T(8,128)(2,1)} %bitcast.6, bf16[256,3456]{1,0:T(8,128)(2,1)} %conv2_in.1, ...), custom_call_target="tpu_custom_call" | custom-call | tf_op jit(solution)/shard_map/pallas_call | solution.py:520
  46.5 1.0 %copy.15 = bf16[1,4,256,512]{3,2,1,0:T(8,128)(2,1)} copy(bf16[1,4,256,512]{3,2,1,0:T(8,128)(2,1)S(1)} %bitcast.4) | data formatting | bytes 2097152
